TPU v7x, 32 devices: a whole 2x2x4 slice. The times are simulated.
32 devices in a mesh: grp: 2 (over x), gx: 8 (over z, y), gy: 2 (over core).
Axes of the slice: x: 2, y: 2, z: 4, core: 2. Of those that a mesh axis runs over, the one named last changes fastest.
Arguments:
- inputs: bfloat16 [1536, 4096], P(('grp', 'gy'), 'gx'), parts along dimension 0, may hold values from -6 to 6
- out_grad: bfloat16 [1536, 4096], P(('grp', 'gy'), 'gx'), parts along dimension 0, may hold values from -3 to 3
- w_gate: bfloat16 [4096, 14336], P('gy', 'gx'), may hold values from -0.125 to 0.125
- w_up: bfloat16 [4096, 14336], P('gy', 'gx'), may hold values from -0.09375 to 0.09375
- w_down: bfloat16 [14336, 4096], P('gx', 'gy'), may hold values from -0.046875 to 0.046875
Outputs:
- in_grad: bfloat16 [1536, 4096], P(('grp', 'gy'), 'gx'), parts along dimension 0
- gate_grad: bfloat16 [8192, 14336], P(('grp', 'gy'), 'gx'), parts along dimension 0
- up_grad: bfloat16 [8192, 14336], P(('grp', 'gy'), 'gx'), parts along dimension 0
- down_grad: bfloat16 [28672, 4096], P(('grp', 'gx'), 'gy'), parts along dimension 0
There are 2 independent parts, one for each index of `grp`. A program takes and returns all parts, laid end to end along the dimension named above; an argument that names none is the same for every part. Nothing has to cross between parts.
All inputs are finite; a program needn't handle non-finite values.
Results may differ from a plain program's by a relative error of at most 0.0059.
Values may be sent and summed in bfloat16 or wider, within the bound.
A program may use at most 256 MiB of HBM per device.

v0:
```python
import jax
import jax.numpy as jnp
from jax import lax
from jax.sharding import PartitionSpec as P


def local_terms(rows_in, rows_grad, gate_w, up_w, down_w):
    gate = jnp.dot(rows_in, gate_w, preferred_element_type=jnp.float32)
    up = jnp.dot(rows_in, up_w, preferred_element_type=jnp.float32)
    sig = jax.nn.sigmoid(gate)
    act = gate * sig
    hidden = (act * up).astype(jnp.bfloat16)
    hidden_grad = jnp.dot(rows_grad, down_w.T, preferred_element_type=jnp.float32)
    up_term = (hidden_grad * act).astype(jnp.bfloat16)
    gate_term = (hidden_grad * up * sig * (1.0 + gate * (1.0 - sig))).astype(jnp.bfloat16)
    return (hidden, gate_term, up_term)


def on_device(inputs, out_grad, w_gate, w_up, w_down):
    rows_in, rows_grad = (
        lax.all_gather(inputs, "gx", axis=1, tiled=True),
        lax.all_gather(out_grad, "gx", axis=1, tiled=True),
    )
    gate_w, up_w = (
        lax.all_gather(w_gate, "gy", axis=0, tiled=True),
        lax.all_gather(w_up, "gy", axis=0, tiled=True),
    )
    down_w = lax.all_gather(w_down, "gy", axis=1, tiled=True)
    hidden, gate_term, up_term = local_terms(rows_in, rows_grad, gate_w, up_w, down_w)
    partial_value = jnp.dot(gate_term, gate_w.T, preferred_element_type=jnp.float32)
    partial_value = partial_value + jnp.dot(up_term, up_w.T, preferred_element_type=jnp.float32)
    in_grad = lax.psum_scatter(partial_value, "gx", scatter_dimension=1, tiled=True)
    gate_part = jnp.dot(rows_in.T, gate_term, preferred_element_type=jnp.float32)
    up_part = jnp.dot(rows_in.T, up_term, preferred_element_type=jnp.float32)
    gate_sum, up_sum = (
        lax.psum_scatter(
            gate_part.astype(jnp.bfloat16), "gy", scatter_dimension=0, tiled=True
        ).astype(jnp.float32),
        lax.psum_scatter(
            up_part.astype(jnp.bfloat16), "gy", scatter_dimension=0, tiled=True
        ).astype(jnp.float32),
    )
    down_part = jnp.dot(hidden.T, rows_grad, preferred_element_type=jnp.float32)
    down_sum = lax.psum_scatter(
        down_part.astype(jnp.bfloat16), "gy", scatter_dimension=1, tiled=True
    )
    return (
        in_grad.astype(jnp.bfloat16),
        gate_sum.astype(jnp.bfloat16),
        up_sum.astype(jnp.bfloat16),
        down_sum,
    )


def solution(mesh):
    in_specs = (
        P(("grp", "gy"), "gx"),
        P(("grp", "gy"), "gx"),
        P("gy", "gx"),
        P("gy", "gx"),
        P("gx", "gy"),
    )
    out_specs = (
        P(("grp", "gy"), "gx"),
        P(("grp", "gy"), "gx"),
        P(("grp", "gy"), "gx"),
        P(("grp", "gx"), "gy"),
    )
    return jax.shard_map(
        on_device, mesh=mesh, in_specs=in_specs, out_specs=out_specs, check_vma=False
    )
```

profile of v0, /device:TPU:0, one launch (start us, length us, event | category | flops | bytes accessed | tf_op | source)
XLA Modules:
  0.0 471.5 jit_solution(18215511641740681626)
XLA Ops:
  7.2 0.0 all-gather.10.cloned.1.call-start
  7.2 0.7 all-gather.10.cloned.1.call-update
  7.9 0.0 all-gather.12.cloned.1.call-start
  7.9 0.7 all-gather.12.cloned.1.call-update
  8.6 0.0 all-gather.14.cloned.1.call-start
  8.7 0.7 all-gather.14.cloned.1.call-update
  9.4 0.0 all-gather.6.cloned.1.call-start
  9.4 0.5 all-gather.6.cloned.1.call-update
  10.0 0.0 all-gather.8.cloned.1.call-start
  10.0 0.5 all-gather.8.cloned.1.call-update
  10.5 0.0 reduce-scatter.5.cloned.1.call-start
  10.6 65.2 %all-gather.10.cloned.1.call-done = bf16[384,4096]{1,0:T(8,128)(2,1)} async-done(((bf16[384,512]{1,0:T(8,128)(2,1)}), bf16[384,4096]{1,0:T(8,128)(2,1)}) %all-gather.10.cloned.1.call-update) | async-done | bytes 3145744 | tf_op jit(solution)/shard_map/all_gather | solution.py:21
  75.8 0.0 copy-start
  75.8 26.8 %all-gather.12.cloned.1.call-done = bf16[4096,1792]{1,0:T(8,128)(2,1)} async-done(((bf16[2048,1792]{1,0:T(8,128)(2,1)}), bf16[4096,1792]{1,0:T(8,128)(2,1)}) %all-gather.12.cloned.1.call-update) | async-done | bytes 14680080 | tf_op jit(solution)/shard_map/all_gather | solution.py:26
  102.6 12.8 %fusion.5 = f32[384,1792]{1,0:T(8,128)} fusion(bf16[384,4096]{1,0:T(8,128)(2,1)} %all-gather.10.cloned.1.call-done, bf16[4096,1792]{1,0:T(8,128)(2,1)} %all-gather.12.cloned.1.call-done), kind=kOutput, calls=%fused_computation.12 | convolution fusion | flops 5637144576 | bytes 20578304 | tf_op jit(solution)/shard_map/dot_general | solution.py:9
  115.4 17.0 %all-gather.14.cloned.1.call-done = bf16[4096,1792]{1,0:T(8,128)(2,1)} async-done(((bf16[2048,1792]{1,0:T(8,128)(2,1)}), bf16[4096,1792]{1,0:T(8,128)(2,1)}) %all-gather.14.cloned.1.call-update) | async-done | bytes 14680080 | tf_op jit(solution)/shard_map/all_gather | solution.py:25
  132.4 0.0 copy-done
  132.5 10.6 %fusion.6 = f32[384,1792]{1,0:T(8,128)} fusion(bf16[384,4096]{1,0:T(8,128)(2,1)S(1)} %copy-done, bf16[4096,1792]{1,0:T(8,128)(2,1)} %all-gather.14.cloned.1.call-done), kind=kOutput, calls=%fused_computation.13 | convolution fusion | flops 5637144576 | bytes 20578304 | tf_op jit(solution)/shard_map/dot_general | solution.py:8
  143.1 55.5 %all-gather.6.cloned.1.call-done = bf16[384,4096]{1,0:T(8,128)(2,1)} async-done(((bf16[384,512]{1,0:T(8,128)(2,1)}), bf16[384,4096]{1,0:T(8,128)(2,1)}) %all-gather.6.cloned.1.call-update) | async-done | bytes 3145744 | tf_op jit(solution)/shard_map/all_gather | solution.py:22
  198.6 26.7 %all-gather.8.cloned.1.call-done = bf16[1792,4096]{1,0:T(8,128)(2,1)} async-done(((bf16[1792,2048]{1,0:T(8,128)(2,1)}), bf16[1792,4096]{1,0:T(8,128)(2,1)}) %all-gather.8.cloned.1.call-update) | async-done | bytes 14680080 | tf_op jit(solution)/shard_map/all_gather | solution.py:28
  225.3 18.4 %multiply_convert_fusion.1 = (bf16[384,1792]{1,0:T(8,128)(2,1)}, bf16[384,1792]{1,0:T(8,128)(2,1)}) fusion(f32[384,1792]{1,0:T(8,128)} %fusion.6, f32[384,1792]{1,0:T(8,128)} %fusion.5, bf16[384,4096]{1,0:T(8,128)(2,1)} %all-gather.6.cloned.1.call-done, bf16[1792,4096]{1,0:T(8,128)(2,1)} %all-gather.8.cloned.1.call-done), kind=kOutput, calls=%fused_computation.7 | convolution fusion | flops 5646090240 | bytes 26083328 | tf_op jit(solution)/shard_map/dot_general | solution.py:13
  243.7 0.0 copy-start.2
  243.7 9.6 %fusion.7 = f32[384,4096]{1,0:T(8,128)S(1)} fusion(bf16[384,1792]{1,0:T(8,128)(2,1)} %get-tuple-element.9, bf16[4096,1792]{1,0:T(8,128)(2,1)} %all-gather.14.cloned.1.call-done), kind=kOutput, calls=%fused_computation.14 | convolution fusion | flops 5637144576 | bytes 22347776 | tf_op jit(solution)/shard_map/dot_general | solution.py:30
  253.3 0.0 copy-done.2
  253.4 11.0 %convolution_add_fusion = f32[384,4096]{1,0:T(8,128)} fusion(f32[384,4096]{1,0:T(8,128)S(1)} %fusion.7, bf16[384,1792]{1,0:T(8,128)(2,1)S(1)} %copy-done.2, bf16[4096,1792]{1,0:T(8,128)(2,1)} %all-gather.12.cloned.1.call-done), kind=kOutput, calls=%fused_computation.5 | convolution fusion | flops 5638717440 | bytes 28639232 | tf_op jit(solution)/shard_map/dot_general | solution.py:31
  264.4 0.0 reduce-scatter.5.cloned.1.call-update
  264.4 0.0 reduce-scatter.9.cloned.1.call-start
  264.4 12.3 %fusion.1 = bf16[4096,1792]{0,1:T(8,128)(2,1)} fusion(bf16[384,1792]{1,0:T(8,128)(2,1)} %get-tuple-element.8, bf16[384,4096]{1,0:T(8,128)(2,1)S(1)} %copy-done), kind=kOutput, calls=%fused_computation.4 | convolution fusion | flops 5644484608 | bytes 19202048 | tf_op jit(solution)/shard_map/dot_general | solution.py:34
  276.8 0.0 reduce-scatter.9.cloned.1.call-update
  276.8 0.0 reduce-scatter.7.cloned.1.call-start
  276.9 12.4 %fusion = bf16[4096,1792]{0,1:T(8,128)(2,1)} fusion(bf16[384,1792]{1,0:T(8,128)(2,1)} %get-tuple-element.9, bf16[384,4096]{1,0:T(8,128)(2,1)S(1)} %copy-done), kind=kOutput, calls=%fused_computation.3 | convolution fusion | flops 5644484608 | bytes 19202048 | tf_op jit(solution)/shard_map/dot_general | solution.py:33
  289.3 0.0 copy-start.1
  289.3 0.0 reduce-scatter.7.cloned.1.call-update
  289.3 0.0 reduce-scatter.11.cloned.1.call-start
  289.3 1.9 copy-done.1
  291.2 13.8 %convolution_convert_fusion = bf16[1792,4096]{1,0:T(8,128)(2,1)} fusion(bf16[384,4096]{1,0:T(8,128)(2,1)S(1)} %copy-done.1, f32[384,1792]{1,0:T(8,128)} %fusion.5, f32[384,1792]{1,0:T(8,128)} %fusion.6), kind=kOutput, calls=%fused_computation | convolution fusion | flops 5648613376 | bytes 23330816 | tf_op jit(solution)/shard_map/dot_general | solution.py:43
  305.1 0.0 reduce-scatter.11.cloned.1.call-update
  305.1 79.0 %reduce-scatter.5.cloned.1.call-done = f32[384,512]{1,0:T(8,128)} async-done(((f32[384,4096]{1,0:T(8,128)}), f32[384,512]{1,0:T(8,128)}) %reduce-scatter.5.cloned.1.call-update) | async-done | bytes 786448 | tf_op jit(solution)/shard_map/reduce_scatter | solution.py:32
  384.1 1.9 convert_element_type.33
  386.0 23.6 %reduce-scatter.9.cloned.1.call-done = bf16[2048,1792]{0,1:T(8,128)(2,1)} async-done(((bf16[4096,1792]{0,1:T(8,128)(2,1)}), bf16[2048,1792]{0,1:T(8,128)(2,1)}) %reduce-scatter.9.cloned.1.call-update) | async-done | bytes 7340048 | tf_op jit(solution)/shard_map/reduce_scatter | solution.py:39
  409.6 9.9 %copy.10 = bf16[2048,1792]{1,0:T(8,128)(2,1)} copy(bf16[2048,1792]{0,1:T(8,128)(2,1)} %reduce-scatter.9.cloned.1.call-done) | data formatting | bytes 14680064
  419.5 17.6 %reduce-scatter.7.cloned.1.call-done = bf16[2048,1792]{0,1:T(8,128)(2,1)} async-done(((bf16[4096,1792]{0,1:T(8,128)(2,1)}), bf16[2048,1792]{0,1:T(8,128)(2,1)}) %reduce-scatter.7.cloned.1.call-update) | async-done | bytes 7340048 | tf_op jit(solution)/shard_map/reduce_scatter | solution.py:36
  437.1 9.9 %copy.9 = bf16[2048,1792]{1,0:T(8,128)(2,1)} copy(bf16[2048,1792]{0,1:T(8,128)(2,1)} %reduce-scatter.7.cloned.1.call-done) | data formatting | bytes 14680064
  447.0 18.0 %reduce-scatter.11.cloned.1.call-done = bf16[1792,2048]{1,0:T(8,128)(2,1)} async-done(((bf16[1792,4096]{1,0:T(8,128)(2,1)}), bf16[1792,2048]{1,0:T(8,128)(2,1)}) %reduce-scatter.11.cloned.1.call-update) | async-done | bytes 7340048 | tf_op jit(solution)/shard_map/reduce_scatter | solution.py:44
Async XLA Ops:
  7.2 68.7 %all-gather.10.cloned.1.call-start = ((), (), s32[]{:S(2)}) async-start(), calls=%async_computation.6 | async-start | bytes 3538944 | tf_op jit(solution)/shard_map/all_gather | solution.py:21
  7.9 94.7 %all-gather.12.cloned.1.call-start = ((), (), s32[]{:S(2)}) async-start(), calls=%async_computation.7 | async-start | bytes 22020096 | tf_op jit(solution)/shard_map/all_gather | solution.py:26
  8.6 123.8 %all-gather.14.cloned.1.call-start = ((), (), s32[]{:S(2)}) async-start(), calls=%async_computation.8 | async-start | bytes 22020096 | tf_op jit(solution)/shard_map/all_gather | solution.py:25
  9.4 189.2 %all-gather.6.cloned.1.call-start = ((), (), s32[]{:S(2)}) async-start(), calls=%async_computation.4 | async-start | bytes 3538944 | tf_op jit(solution)/shard_map/all_gather | solution.py:22
  10.0 215.3 %all-gather.8.cloned.1.call-start = ((), (), s32[]{:S(2)}) async-start(), calls=%async_computation.5 | async-start | bytes 22020096 | tf_op jit(solution)/shard_map/all_gather | solution.py:28
  10.5 373.6 %reduce-scatter.5.cloned.1.call-start = ((), (), s32[]{:S(2)}) async-start(), calls=%async_computation.9 | async-start | bytes 7077888 | tf_op jit(solution)/shard_map/reduce_scatter | solution.py:32
  75.8 56.6 %copy-start = (bf16[384,4096]{1,0:T(8,128)(2,1)S(1)}, bf16[384,4096]{1,0:T(8,128)(2,1)}, u32[]{:S(2)}) copy-start(bf16[384,4096]{1,0:T(8,128)(2,1)} %all-gather.10.cloned.1.call-done) | copy-start | bytes 9437188
  243.7 9.6 %copy-start.2 = (bf16[384,1792]{1,0:T(8,128)(2,1)S(1)}, bf16[384,1792]{1,0:T(8,128)(2,1)}, u32[]{:S(2)}) copy-start(bf16[384,1792]{1,0:T(8,128)(2,1)} %get-tuple-element.8) | copy-start | bytes 4128772
  264.4 145.2 %reduce-scatter.9.cloned.1.call-start = ((), (), s32[]{:S(2)}) async-start(), calls=%async_computation.11 | async-start | bytes 22020096 | tf_op jit(solution)/shard_map/reduce_scatter | solution.py:39
  276.8 160.3 %reduce-scatter.7.cloned.1.call-start = ((), (), s32[]{:S(2)}) async-start(), calls=%async_computation.10 | async-start | bytes 22020096 | tf_op jit(solution)/shard_map/reduce_scatter | solution.py:36
  289.3 2.0 copy-start.1
  289.3 175.7 %reduce-scatter.11.cloned.1.call-start = ((), (), s32[]{:S(2)}) async-start(), calls=%async_computation.12 | async-start | bytes 22020096 | tf_op jit(solution)/shard_map/reduce_scatter | solution.py:44
Sparse Core Ops, SparseCore 0:
  10.0 65.7 all-gather.9
  77.4 25.2 all-gather.11
  104.2 28.1 all-gather.13
  134.3 64.2 all-gather.5
  200.0 25.2 all-gather.7
  264.5 119.5 reduce-scatter.4
  386.4 23.1 reduce-scatter.8
  411.9 25.1 reduce-scatter.6
  440.0 24.9 reduce-scatter.10
where the time goes:
time: 472 us
  waiting for transfers between devices  333 us (71%)
  matrix products  101 us (21%)
  local copies, waits for them, and re-layouts  21.7 us (5%)
  between operations  13.9 us (3%)
    reduce_scatter x1, waiting for transfers between devices, on_device(): lax.psum_scatter(partial_value, 'gx', scatter_dimension=1, tiled=True)  79 us
    all_gather x1, waiting for transfers between devices, on_device(): lax.all_gather(inputs, 'gx', axis=1, tiled=True)  65.2 us
    all_gather x1, waiting for transfers between devices, on_device(): lax.all_gather(out_grad, 'gx', axis=1, tiled=True)  55.5 us
    all_gather x1, waiting for transfers between devices, on_device(): lax.all_gather(w_up, 'gy', axis=0, tiled=True)  26.8 us
    all_gather x1, waiting for transfers between devices, on_device(): down_w = lax.all_gather(w_down, 'gy', axis=1, tiled=True)  26.7 us
    reduce_scatter x1, waiting for transfers between devices, on_device(): lax.psum_scatter(up_part.astype(jnp.bfloat16), 'gy', scatter_dimension=0,...  23.6 us
    unnamed x8, local copies, waits for them, and re-layouts  21.7 us
    dot_general x1, matrix products, local_terms(): jnp.dot(rows_grad, down_w.T, preferred_element_type=jnp.float32)  18.4 us
  transfers between devices with their start and end apart: 9, of which 9 were waited for; matrix products, arithmetic and copies ran while one was open for 18% of the time, Pallas kernels for 0%

commit v1 on v0

v1 whole, which is shorter than its diff:
```python
import functools

import jax
import jax.numpy as jnp
from jax import lax
from jax.experimental import pallas as pl
from jax.experimental.pallas import tpu as pltpu
from jax.sharding import PartitionSpec as P

MESH = pl.DeviceIdType.MESH
F32 = jnp.float32
BF16 = jnp.bfloat16


def ring_place(n, me):
    if n > 8:
        return me
    up, side = me // 2, me % 2
    return (1 - side) * up + side * (n - 1 - up)


def ring_member(n, place):
    if n > 8:
        return place
    late = place // (n // 2)
    return (1 - late) * 2 * place + late * (2 * (n - 1 - place) + 1)


def terms_kernel(n, tiles, width, x_in, g_in, wg, wu, wd, hid, gt, ut, x_out, g_out,
                 xb, gb, wgu, wdb, a_own, a_got, b_own, b_got,
                 in_sem, wgu_sem, wd_sem, ring_send, ring_recv, sib_send, sib_recv,
                 part_send, part_recv, out_sem, credit):
    half = n // 2
    me, t = lax.axis_index("gx"), lax.axis_index("gy")
    sib = 1 - t
    place = ring_place(n, me)
    right = ring_member(n, lax.rem(place + 1, n))
    left = ring_member(n, lax.rem(place + n - 1, n))
    dl = xb.shape[-1]
    rows = 4 * xb.shape[-2]

    def own_in(arr, c):
        src, buf = ((x_in, xb), (g_in, gb))[arr]
        return pltpu.make_async_copy(src.at[c], buf.at[me, t, c], in_sem.at[arr, c])

    for arr in range(2):
        for c in range(2):
            own_in(arr, c).start()

    barrier = pltpu.get_barrier_semaphore()
    pl.semaphore_signal(barrier, inc=1, device_id={"gx": left}, device_id_type=MESH)
    pl.semaphore_signal(barrier, inc=1, device_id={"gx": right}, device_id_type=MESH)
    pl.semaphore_signal(barrier, inc=1, device_id={"gy": sib}, device_id_type=MESH)
    pl.semaphore_wait(barrier, 3)

    def hop(arr, j, s, c, way):
        buf = (xb, gb)[arr]
        return pltpu.make_async_remote_copy(
            src_ref=buf.at[j, t, c], dst_ref=buf.at[j, t, c],
            send_sem=ring_send.at[arr, s - 1, c, way], recv_sem=ring_recv.at[arr, s - 1, c, way],
            device_id={"gx": (right, left)[way]}, device_id_type=MESH)

    def across(arr, j, c, whose):
        buf = (xb, gb)[arr]
        return pltpu.make_async_remote_copy(
            src_ref=buf.at[j, whose, c], dst_ref=buf.at[j, whose, c],
            send_sem=sib_send.at[arr, j % half, c], recv_sem=sib_recv.at[arr, j % half, c],
            device_id={"gy": sib}, device_id_type=MESH)

    def to_sibling(arr, j, c):
        @pl.when(j // half != t)
        def _():
            across(arr, j, c, t).start()

    def source(s, way):
        return ring_member(n, lax.rem(place + n + (s if way else -s), n))

    def begin(arr):
        for c in range(2):
            own_in(arr, c).wait()
            for way in range(2):
                hop(arr, me, 1, c, way).start()
            to_sibling(arr, me, c)

    def event(arr, e):
        s, c = 1 + e // 2, e % 2
        for way in range(2):
            j = source(s, way)
            hop(arr, j, s, c, way).wait_recv()

            @pl.when((s + 1 < half) | (c == way))
            def _():
                hop(arr, j, s + 1, c, way).start()

            to_sibling(arr, j, c)

    def last_event(arr):
        for way in range(2):
            j = source(half, way)
            hop(arr, j, half, way, way).wait_recv()
            to_sibling(arr, j, way)

    def from_sibling(arr):
        def one(k, carry):
            for c in range(2):
                across(arr, t * half + k, c, sib).wait_recv()
            return carry
        lax.fori_loop(0, half, one, 0)

    def weights(i, which):
        return pltpu.make_async_copy(
            (wg, wu)[which].at[:, pl.ds(pl.multiple_of(i * width, 128), width)],
            wgu.at[i % 2, which], wgu_sem.at[i % 2, which])

    def down(i):
        return pltpu.make_async_copy(
            wd.at[pl.ds(pl.multiple_of(i * width, 16), width), :], wdb.at[i], wd_sem.at[i])

    def part(which, i):
        src, dst = ((a_own, a_got), (b_own, b_got), (a_got, b_got))[which]
        return pltpu.make_async_remote_copy(
            src_ref=src.at[i], dst_ref=dst.at[i],
            send_sem=part_send.at[which, i], recv_sem=part_recv.at[which, i],
            device_id={"gy": sib}, device_id_type=MESH)

    begin(0)
    for i in range(min(2, tiles)):
        weights(i, 0).start()
        weights(i, 1).start()
    for i in range(tiles):
        down(i).start()

    def x_step(e, carry):
        event(0, e)
        return carry
    lax.fori_loop(0, 2 * (half - 1), x_step, 0)
    begin(1)
    last_event(0)
    from_sibling(0)

    def first_half(i):
        at = pl.ds(pl.multiple_of(i * width, 128), width)
        part(0, i).wait()
        part(1, i).wait()
        gate = a_own[i] + a_got[i]
        up = b_own[i] + b_got[i]
        sig = 1.0 / (1.0 + jnp.exp(-gate))
        act = gate * sig
        hid[:, at] = (act * up).astype(BF16)
        a_own[i] = act
        b_own[i] = up * sig * (1.0 + gate * (1.0 - sig))

    def tile(i):
        for which, own in ((0, a_own), (1, b_own)):
            weights(i, which).wait()
            total = None
            for k in range(half):
                lhs = xb[t * half + k].reshape(rows, dl)
                term = jnp.dot(lhs, wgu[i % 2, which, k * dl:(k + 1) * dl, :], preferred_element_type=F32)
                total = term if total is None else total + term
            own[i] = total
            part(which, i).start()

            @pl.when(i + 2 < tiles)
            def _():
                weights(i + 2, which).start()

        @pl.when(i > 0)
        def _():
            first_half(i - 1)

    def g_step(e, carry):
        event(1, e)

        @pl.when(e < tiles)
        def _():
            tile(e)
        return carry
    lax.fori_loop(0, 2 * (half - 1), g_step, 0)
    last_event(1)

    def rest(i, carry):
        tile(i)
        return carry
    lax.fori_loop(min(2 * (half - 1), tiles), tiles, rest, 0)
    first_half(tiles - 1)
    pl.semaphore_signal(credit, inc=1, device_id={"gy": sib}, device_id_type=MESH)
    from_sibling(1)

    def outs(arr, k):
        buf, out = ((xb, x_out), (gb, g_out))[arr]
        return pltpu.make_async_copy(
            buf.at[t * half + k], out.at[:, :, :, pl.ds(k * dl, dl)], out_sem.at[arr, k])

    for arr in range(2):
        for k in range(half):
            outs(arr, k).start()
    pl.semaphore_wait(credit, 1)

    def second_half(i):
        at = pl.ds(pl.multiple_of(i * width, 128), width)
        part(2, i).wait_recv()
        grad = a_got[i] + b_got[i]
        ut[:, at] = (grad * a_own[i]).astype(BF16)
        gt[:, at] = (grad * b_own[i]).astype(BF16)

    def grad_tile(i, carry):
        down(i).wait()
        total = None
        for k in range(half):
            lhs = gb[t * half + k].reshape(rows, dl)
            term = lax.dot_general(lhs, wdb[i, :, k * dl:(k + 1) * dl], (((1,), (1,)), ((), ())),
                                   preferred_element_type=F32)
            total = term if total is None else total + term
        a_got[i] = total
        part(2, i).start()

        @pl.when(i > 0)
        def _():
            second_half(i - 1)
        return carry
    lax.fori_loop(0, tiles, grad_tile, 0)
    second_half(tiles - 1)

    def sent(i, carry):
        part(2, i).wait_send()
        return carry
    lax.fori_loop(0, tiles, sent, 0)

    for arr in range(2):
        for k in range(half):
            outs(arr, k).wait()

        def crossed(k, carry):
            for c in range(2):
                across(arr, sib * half + k, c, t).wait_send()
            return carry
        lax.fori_loop(0, half, crossed, 0)

        def hopped(s, carry):
            for c in range(2):
                for way in range(2):
                    hop(arr, me, s, c, way).wait_send()
            return carry
        lax.fori_loop(1, half, hopped, 0)
        for way in range(2):
            hop(arr, me, half, way, way).wait_send()


def terms(n, inputs, out_grad, w_gate, w_up, w_down):
    tok, dl = inputs.shape
    dh, ff = w_gate.shape
    half = n // 2
    width = 256 if ff % 256 == 0 else ff
    tiles = ff // width
    anyspace = pl.BlockSpec(memory_space=pl.ANY)
    vmem = pl.BlockSpec(memory_space=pltpu.VMEM)
    quarter = tok // 2
    term = jax.ShapeDtypeStruct((2 * tok, ff), BF16)
    gathered = jax.ShapeDtypeStruct((2, 2, quarter, dh), BF16)
    dma = pltpu.SemaphoreType.DMA
    return pl.pallas_call(
        functools.partial(terms_kernel, n, tiles, width),
        out_shape=(term, term, term, gathered, gathered),
        in_specs=[anyspace] * 5,
        out_specs=(vmem, vmem, vmem, anyspace, anyspace),
        scratch_shapes=[
            pltpu.VMEM((n, 2, 2, quarter, dl), BF16),
            pltpu.VMEM((n, 2, 2, quarter, dl), BF16),
            pltpu.VMEM((2, 2, dh, width), BF16),
            pltpu.VMEM((tiles, width, dh), BF16),
            pltpu.VMEM((tiles, 2 * tok, width), F32),
            pltpu.VMEM((tiles, 2 * tok, width), F32),
            pltpu.VMEM((tiles, 2 * tok, width), F32),
            pltpu.VMEM((tiles, 2 * tok, width), F32),
            dma((2, 2)),
            dma((2, 2)),
            dma((tiles,)),
            dma((2, half, 2, 2)),
            dma((2, half, 2, 2)),
            dma((2, half, 2)),
            dma((2, half, 2)),
            dma((3, tiles)),
            dma((3, tiles)),
            dma((2, half)),
            pltpu.SemaphoreType.REGULAR,
        ],
        compiler_params=pltpu.CompilerParams(
            collective_id=0, has_side_effects=True, vmem_limit_bytes=62 * 1024 * 1024),
        cost_estimate=pl.CostEstimate(
            flops=12 * tok * dh * ff, bytes_accessed=10 * dh * ff, transcendentals=2 * tok * ff),
    )(inputs.reshape(2, quarter, dl), out_grad.reshape(2, quarter, dl), w_gate, w_up, w_down)


def reduce_ring(n, blocks, me):
    half = n // 2
    members = [int(ring_member(n, p)) for p in range(n)]
    ways = [
        [(members[p], members[(p + 1) % n]) for p in range(n)],
        [(members[p], members[(p - 1) % n]) for p in range(n)],
    ]
    place = ring_place(n, me)
    got = [None, None]
    for s in range(half):
        for way in range(2):
            d = half - s
            block = blocks(ring_member(n, (place + n + (-d if way else d)) % n))
            rows = block.shape[0]
            if s == 0:
                block = block[way * rows // 2:(way + 1) * rows // 2]
            elif s == 1:
                pad = (0, rows // 2) if way == 0 else (rows // 2, 0)
                block = block + jnp.pad(got[way].astype(F32), (pad, (0, 0)))
            else:
                block = block + got[way].astype(F32)
            got[way] = lax.ppermute(block.astype(BF16), "gx", ways[way])
    return (blocks(me) + got[0].astype(F32) + got[1].astype(F32)).astype(BF16)


def on_device(n, inputs, out_grad, w_gate, w_up, w_down):
    tok, dl = inputs.shape
    dh, ff = w_gate.shape
    half = n // 2
    me, t = lax.axis_index("gx"), lax.axis_index("gy")
    hid, gt, ut, xh, gh = terms(n, inputs, out_grad, w_gate, w_up, w_down)
    xh, gh = xh.reshape(2 * tok, dh), gh.reshape(2 * tok, dh)

    def back(rows):
        a = lax.dynamic_slice_in_dim(gt, rows * tok, tok, 0)
        b = lax.dynamic_slice_in_dim(ut, rows * tok, tok, 0)
        nt = (((1,), (1,)), ((), ()))
        return lax.dot_general(a, w_gate, nt, preferred_element_type=F32) + lax.dot_general(
            b, w_up, nt, preferred_element_type=F32)

    theirs = lax.ppermute(back(1 - t).astype(BF16), "gy", [(0, 1), (1, 0)])
    mine = back(t)

    def blocks(q):
        at = (q % half) * dl
        own = lax.dynamic_slice_in_dim(mine, at, dl, 1)
        other = lax.dynamic_slice_in_dim(theirs, at, dl, 1).astype(F32)
        return jnp.where(q // half == t, own, other)

    in_grad = reduce_ring(n, blocks, me)
    tn = (((0,), (0,)), ((), ()))
    gate_grad = lax.dot_general(xh, gt, tn, preferred_element_type=F32).astype(BF16)
    up_grad = lax.dot_general(xh, ut, tn, preferred_element_type=F32).astype(BF16)
    down_grad = lax.dot_general(hid, gh, tn, preferred_element_type=F32).astype(BF16)
    return in_grad, gate_grad, up_grad, down_grad


def solution(mesh):
    in_specs = (
        P(("grp", "gy"), "gx"),
        P(("grp", "gy"), "gx"),
        P("gy", "gx"),
        P("gy", "gx"),
        P("gx", "gy"),
    )
    out_specs = (
        P(("grp", "gy"), "gx"),
        P(("grp", "gy"), "gx"),
        P(("grp", "gy"), "gx"),
        P(("grp", "gx"), "gy"),
    )
    return jax.shard_map(
        functools.partial(on_device, mesh.shape["gx"]),
        mesh=mesh, in_specs=in_specs, out_specs=out_specs, check_vma=False
    )
```

time: 472 us -> 189 us (0.40)
  waiting for transfers between devices: 333 us -> 22.5 us
  Pallas kernels: 0 us -> 92 us
  matrix products: 101 us -> 51.1 us
  local copies, waits for them, and re-layouts: 21.7 us -> 0.54 us
  between operations: 13.9 us -> 0.74 us
  other arithmetic: 1.93 us -> 12.9 us
  starting transfers between devices: 0.35 us -> 8.73 us
    all_gather x5 -> x0, waiting for transfers between devices: 191 us -> none  [the longest x1 65.2 us: on_device(): lax.all_gather(inputs, 'gx', axis=1, tiled=True)]
    reduce_scatter x4 -> x0, waiting for transfers between devices: 138 us -> none  [the longest x1 79 us: on_device(): lax.psum_scatter(partial_value, 'gx', scatter_dimension=1, tiled=True)]
    pallas_call x0 -> x1, Pallas kernels: none -> 92 us  [terms(): pl.pallas_call(functools.partial(terms_kernel, n, tiles, width), out_shap...]
    dot_general x8 -> x7, matrix products: 101 us -> 51.1 us  [the longest x2 11.3 us: back(): lax.dot_general(a, w_gate, nt, preferred_element_type=F32)]
    ppermute x0 -> x9, waiting for transfers between devices: none -> 22.5 us  [the longest x8 22.5 us: reduce_ring(): got[way] = lax.ppermute(block.astype(BF16), 'gx', ways[way])]
    unnamed x8 -> x10, local copies, waits for them, and re-layouts: 21.7 us -> 0.54 us
    convert_element_type x1 -> x6, other arithmetic: 1.93 us -> 11.1 us  [the longest x5 8.88 us: reduce_ring(): got[way] = lax.ppermute(block.astype(BF16), 'gx', ways[way])]
    ppermute x0 -> x9, starting transfers between devices: none -> 8.73 us  [the longest x8 8.57 us: reduce_ring(): got[way] = lax.ppermute(block.astype(BF16), 'gx', ways[way])]
  transfers between devices with their start and end apart: 9 -> 9, of which waited for: 9 -> 4; matrix products, arithmetic and copies ran while one was open for 18% -> 23% of each run, Pallas kernels for 0% -> 0%
where the time goes in v1:
time: 189 us
  Pallas kernels  92 us (49%)
  matrix products  51.1 us (27%)
  waiting for transfers between devices  22.5 us (12%)
  other arithmetic  12.9 us (7%)
  starting transfers between devices  8.73 us (5%)
    pallas_call x1, Pallas kernels, terms(): pl.pallas_call(functools.partial(terms_kernel, n, tiles, width), out_shap...  92 us
    ppermute x8, waiting for transfers between devices, reduce_ring(): got[way] = lax.ppermute(block.astype(BF16), 'gx', ways[way])  22.5 us
    dot_general x2, matrix products, back(): lax.dot_general(a, w_gate, nt, preferred_element_type=F32)  11.3 us
    dot_general x1, matrix products, on_device(): lax.dot_general(xh, gt, tn, preferred_element_type=F32).astype(BF16)  10.3 us
    dot_general x1, matrix products, on_device(): lax.dot_general(hid, gh, tn, preferred_element_type=F32).astype(BF16)  10.2 us
    dot_general x1, matrix products, on_device(): lax.dot_general(xh, ut, tn, preferred_element_type=F32).astype(BF16)  9.85 us
    dot_general x2, matrix products, back(): lax.dot_general(b, w_up, nt, preferred_element_type=F32)  9.45 us
    convert_element_type x5, other arithmetic, reduce_ring(): got[way] = lax.ppermute(block.astype(BF16), 'gx', ways[way])  8.88 us
  transfers between devices with their start and end apart: 9, of which 4 were waited for; matrix products, arithmetic and copies ran while one was open for 23% of the time, Pallas kernels for 0%

profile of v1, /device:TPU:0, one launch (start us, length us, event | category | flops | bytes accessed | tf_op | source)
XLA Modules:
  0.0 188.5 jit_solution(3448443755262733550)
XLA Ops:
  0.6 92.0 %shard_map.84 = (bf16[768,1792]{1,0:T(8,128)(2,1)}, bf16[768,1792]{1,0:T(8,128)(2,1)}, bf16[768,1792]{1,0:T(8,128)(2,1)}, bf16[2,2,192,2048]{3,2,1,0:T(8,128)(2,1)}, bf16[2,2,192,2048]{3,2,1,0:T(8,128)(2,1)}) custom-call(bf16[2,192,512]{2,1,0:T(8,128)(2,1)} %bitcast.14, bf16[2,192,512]{2,1,0:T(8,128)(2,1)} %bitcast.15, bf16[2048,1792]{1,0:T(8,128)(2,1)} %wg.1, ...), custom_call_target="tpu_custom_call" | custom-call | flops 16911433728 | bytes 36700160 | tf_op jit(solution)/shard_map/pallas_call | solution.py:262
  92.6 0.0 copy-start
  92.7 0.0 copy-start.2
  92.7 5.9 %fusion.1 = f32[384,2048]{1,0:T(8,128)S(1)} fusion(bf16[2048,1792]{1,0:T(8,128)(2,1)} %wg.1, bf16[768,1792]{1,0:T(8,128)(2,1)} %get-tuple-element.9, s32[]{:T(128)S(6)} %select_n.235), kind=kOutput, calls=%fused_computation.6 | convolution fusion | flops 2818572288 | bytes 11862020 | tf_op jit(solution)/shard_map/dot_general | solution.py:332
  98.5 0.0 copy-done
  98.6 0.5 copy-done.2
  99.1 0.0 copy-start.4
  99.1 4.1 %add_convert_fusion = bf16[384,2048]{1,0:T(8,128)(2,1)} fusion(f32[384,2048]{1,0:T(8,128)S(1)} %fusion.1, bf16[2048,1792]{1,0:T(8,128)(2,1)S(1)} %copy-done, bf16[768,1792]{1,0:T(8,128)(2,1)S(1)} %copy-done.2, s32[]{:T(128)S(6)} %select_n.235), kind=kOutput, calls=%fused_computation.3 | convolution fusion | flops 2820145152 | bytes 13434884 | tf_op jit(solution)/shard_map/dot_general | solution.py:332
  103.2 0.2 collective-permute-start
  103.4 0.0 copy-done.4
  103.4 0.0 copy-start.3
  103.4 5.4 %fusion.4 = f32[384,2048]{1,0:T(8,128)S(1)} fusion(bf16[2048,1792]{1,0:T(8,128)(2,1)} %wg.1, bf16[768,1792]{1,0:T(8,128)(2,1)S(1)} %copy-done.4, s32[]{:T(128)S(6)} %select_n.232), kind=kOutput, calls=%fused_computation.9 | convolution fusion | flops 2818572288 | bytes 11862020 | tf_op jit(solution)/shard_map/dot_general | solution.py:332
  108.8 0.0 copy-done.3
  108.8 5.3 %convolution_add_fusion = f32[384,2048]{1,0:T(8,128)S(1)} fusion(f32[384,2048]{1,0:T(8,128)S(1)} %fusion.4, bf16[2048,1792]{1,0:T(8,128)(2,1)} %wu.1, bf16[768,1792]{1,0:T(8,128)(2,1)S(1)} %copy-done.3, s32[]{:T(128)S(6)} %select_n.232), kind=kOutput, calls=%fused_computation.4 | convolution fusion | flops 2819358720 | bytes 15007748 | tf_op jit(solution)/shard_map/dot_general | solution.py:332
  114.2 0.0 collective-permute-done
  114.2 1.8 fusion.7
  116.0 1.6 collective-permute-start.1
  117.6 5.7 %collective-permute-done.1 = bf16[192,512]{1,0:T(8,128)(2,1)} collective-permute-done((bf16[192,512]{1,0:T(8,128)(2,1)S(1)}, bf16[192,512]{1,0:T(8,128)(2,1)}, u32[]{:S(2)}, u32[]{:S(2)}) %collective-permute-start.1) | collective-permute-done | bytes 196640 | tf_op jit(solution)/shard_map/ppermute | solution.py:316
  123.3 1.2 add_convert_fusion.7
  124.5 1.6 collective-permute-start.2
  126.2 9.1 %collective-permute-done.2 = bf16[384,512]{1,0:T(8,128)(2,1)} collective-permute-done((bf16[384,512]{1,0:T(8,128)(2,1)S(1)}, bf16[384,512]{1,0:T(8,128)(2,1)}, u32[]{:S(2)}, u32[]{:S(2)}) %collective-permute-start.2) | collective-permute-done | bytes 393248 | tf_op jit(solution)/shard_map/ppermute | solution.py:316
  135.2 1.3 add_convert_fusion.6
  136.5 1.7 collective-permute-start.3
  138.2 0.4 collective-permute-start.5
  138.6 0.0 copy-start.1
  138.6 5.6 %collective-permute-done.5 = bf16[192,512]{1,0:T(8,128)(2,1)} collective-permute-done((bf16[192,512]{1,0:T(8,128)(2,1)}, bf16[192,512]{1,0:T(8,128)(2,1)}, u32[]{:S(2)}, u32[]{:S(2)}) %collective-permute-start.5) | collective-permute-done | bytes 196640 | tf_op jit(solution)/shard_map/ppermute | solution.py:316
  144.2 2.2 %collective-permute-done.3 = bf16[384,512]{1,0:T(8,128)(2,1)} collective-permute-done((bf16[384,512]{1,0:T(8,128)(2,1)S(1)}, bf16[384,512]{1,0:T(8,128)(2,1)}, u32[]{:S(2)}, u32[]{:S(2)}) %collective-permute-start.3) | collective-permute-done | bytes 393248 | tf_op jit(solution)/shard_map/ppermute | solution.py:316
  146.3 2.3 %add_convert_fusion.5 = (bf16[384,512]{1,0:T(8,128)(2,1)S(1)}, bf16[384,512]{1,0:T(8,128)(2,1)}) fusion(bf16[384,512]{1,0:T(8,128)(2,1)} %collective-permute-done.3, f32[384,2048]{1,0:T(8,128)S(1)} %convolution_add_fusion, s32[]{:T(128)S(6)} %select_n.244, bf16[384,2048]{1,0:T(8,128)(2,1)} %collective-permute-done, pred[]{:T(512)S(6)} %eq.47, ...), kind=kLoop, calls=%fused_computation.15 | loop fusion | flops 1966080 | bytes 3735562 | tf_op jit(solution)/shard_map/convert_element_type | solution.py:316
  148.7 0.5 collective-permute-start.6
  149.1 0.0 copy-done.1
  149.1 9.9 %convolution_convert_fusion.1 = bf16[2048,1792]{1,0:T(8,128)(2,1)} fusion(bf16[768,2048]{1,0:T(8,128)(2,1)S(1)} %bitcast.18, bf16[768,1792]{1,0:T(8,128)(2,1)} %get-tuple-element.10), kind=kOutput, calls=%fused_computation.1 | convolution fusion | flops 5640814592 | bytes 13238272 | tf_op jit(solution)/shard_map/dot_general | solution.py:347
  159.0 0.0 collective-permute-done.6
  159.0 2.0 %add_convert_fusion.3 = bf16[384,512]{1,0:T(8,128)(2,1)} fusion(bf16[384,512]{1,0:T(8,128)(2,1)} %collective-permute-done.6, f32[384,2048]{1,0:T(8,128)S(1)} %convolution_add_fusion, s32[]{:T(128)S(6)} %select_n.279, bf16[384,2048]{1,0:T(8,128)(2,1)} %collective-permute-done, pred[]{:T(512)S(6)} %eq.52), kind=kLoop, calls=%fused_computation.13 | loop fusion | flops 983040 | bytes 1966085 | tf_op jit(solution)/shard_map/convert_element_type | solution.py:316
  161.0 0.8 collective-permute-start.7
  161.8 10.3 %convolution_convert_fusion.2 = bf16[2048,1792]{1,0:T(8,128)(2,1)} fusion(bf16[768,2048]{1,0:T(8,128)(2,1)} %bitcast.17, bf16[768,1792]{1,0:T(8,128)(2,1)} %get-tuple-element.9), kind=kOutput, calls=%fused_computation.2 | convolution fusion | flops 5640814592 | bytes 13238272 | tf_op jit(solution)/shard_map/dot_general | solution.py:346
  172.0 1.3 collective-permute-start.4
  173.3 0.0 collective-permute-done.7
  173.3 2.0 %add_convert_fusion.2 = bf16[384,512]{1,0:T(8,128)(2,1)} fusion(bf16[384,512]{1,0:T(8,128)(2,1)} %collective-permute-done.7, f32[384,2048]{1,0:T(8,128)S(1)} %convolution_add_fusion, s32[]{:T(128)S(6)} %select_n.272, bf16[384,2048]{1,0:T(8,128)(2,1)} %collective-permute-done, pred[]{:T(512)S(6)} %eq.51), kind=kLoop, calls=%fused_computation.12 | loop fusion | flops 983040 | bytes 1966085 | tf_op jit(solution)/shard_map/convert_element_type | solution.py:316
  175.3 0.8 collective-permute-start.8
  176.1 10.2 %convolution_convert_fusion = bf16[1792,2048]{1,0:T(8,128)(2,1)} fusion(bf16[768,1792]{1,0:T(8,128)(2,1)} %get-tuple-element.12, bf16[768,2048]{1,0:T(8,128)(2,1)} %bitcast.16), kind=kOutput, calls=%fused_computation | convolution fusion | flops 5640814592 | bytes 13238272 | tf_op jit(solution)/shard_map/dot_general | solution.py:348
  186.3 0.0 collective-permute-done.4
  186.3 0.0 collective-permute-done.8
  186.3 2.2 %add_convert_fusion.1 = bf16[384,512]{1,0:T(8,128)(2,1)} fusion(bf16[384,512]{1,0:T(8,128)(2,1)} %collective-permute-done.8, bf16[384,512]{1,0:T(8,128)(2,1)} %collective-permute-done.4, f32[384,2048]{1,0:T(8,128)S(1)} %convolution_add_fusion, s32[]{:T(128)S(6)} %select_n.234, bf16[384,2048]{1,0:T(8,128)(2,1)} %collective-permute-done, pred[]{:T(512)S(6)} %eq.46), kind=kLoop, calls=%fused_computation.11 | loop fusion | flops 1376256 | bytes 2359301 | tf_op jit(solution)/shard_map/convert_element_type | solution.py:317
Async XLA Ops:
  92.6 5.9 %copy-start = (bf16[2048,1792]{1,0:T(8,128)(2,1)S(1)}, bf16[2048,1792]{1,0:T(8,128)(2,1)}, u32[]{:S(2)}) copy-start(bf16[2048,1792]{1,0:T(8,128)(2,1)} %wu.1) | copy-start | bytes 22020100
  92.7 6.4 %copy-start.2 = (bf16[768,1792]{1,0:T(8,128)(2,1)S(1)}, bf16[768,1792]{1,0:T(8,128)(2,1)}, u32[]{:S(2)}) copy-start(bf16[768,1792]{1,0:T(8,128)(2,1)} %get-tuple-element.10) | copy-start | bytes 8257540
  99.1 4.3 %copy-start.4 = (bf16[768,1792]{1,0:T(8,128)(2,1)S(1)}, bf16[768,1792]{1,0:T(8,128)(2,1)}, u32[]{:S(2)}) copy-start(bf16[768,1792]{1,0:T(8,128)(2,1)} %get-tuple-element.9) | copy-start | bytes 8257540
  103.2 11.0 %collective-permute-start = (bf16[384,2048]{1,0:T(8,128)(2,1)}, bf16[384,2048]{1,0:T(8,128)(2,1)}, u32[]{:S(2)}, u32[]{:S(2)}) collective-permute-start(bf16[384,2048]{1,0:T(8,128)(2,1)} %add_convert_fusion), channel_id=1, source_target_pairs={{0,1},{1,0},{2,3},{3,2},{4,5},{5,4},{6,7},{7,6},{8,9},{9,8},{10,11... | collective-permute-start | bytes 4718600 | tf_op jit(solution)/shard_map/ppermute | solution.py:335
  103.4 5.5 %copy-start.3 = (bf16[768,1792]{1,0:T(8,128)(2,1)S(1)}, bf16[768,1792]{1,0:T(8,128)(2,1)}, u32[]{:S(2)}) copy-start(bf16[768,1792]{1,0:T(8,128)(2,1)} %get-tuple-element.10) | copy-start | bytes 8257540
  116.0 7.3 %collective-permute-start.1 = (bf16[192,512]{1,0:T(8,128)(2,1)S(1)}, bf16[192,512]{1,0:T(8,128)(2,1)}, u32[]{:S(2)}, u32[]{:S(2)}) collective-permute-start(bf16[192,512]{1,0:T(8,128)(2,1)S(1)} %get-tuple-element.16), channel_id=1, source_target_pairs={{0,4},{4,8},{8,12},{12,14},{14,10},{10,6},{6,2},{2,0},{1,5},{5,9},... | collective-permute-start | bytes 589832 | tf_op jit(solution)/shard_map/ppermute | solution.py:316
  124.5 10.7 %collective-permute-start.2 = (bf16[384,512]{1,0:T(8,128)(2,1)S(1)}, bf16[384,512]{1,0:T(8,128)(2,1)}, u32[]{:S(2)}, u32[]{:S(2)}) collective-permute-start(bf16[384,512]{1,0:T(8,128)(2,1)S(1)} %add_convert_fusion.7), channel_id=1, source_target_pairs={{0,4},{4,8},{8,12},{12,14},{14,10},{10,6},{6,2},{2,0},{1,5},{5,9},... | collective-permute-start | bytes 1179656 | tf_op jit(solution)/shard_map/ppermute | solution.py:316
  136.5 9.8 %collective-permute-start.3 = (bf16[384,512]{1,0:T(8,128)(2,1)S(1)}, bf16[384,512]{1,0:T(8,128)(2,1)}, u32[]{:S(2)}, u32[]{:S(2)}) collective-permute-start(bf16[384,512]{1,0:T(8,128)(2,1)S(1)} %add_convert_fusion.6), channel_id=1, source_target_pairs={{0,4},{4,8},{8,12},{12,14},{14,10},{10,6},{6,2},{2,0},{1,5},{5,9},... | collective-permute-start | bytes 1179656 | tf_op jit(solution)/shard_map/ppermute | solution.py:316
  138.2 6.0 %collective-permute-start.5 = (bf16[192,512]{1,0:T(8,128)(2,1)}, bf16[192,512]{1,0:T(8,128)(2,1)}, u32[]{:S(2)}, u32[]{:S(2)}) collective-permute-start(bf16[192,512]{1,0:T(8,128)(2,1)} %get-tuple-element.17), channel_id=1, source_target_pairs={{0,2},{4,0},{8,4},{12,8},{14,12},{10,14},{6,10},{2,6},{1,3},{5,1},... | collective-permute-start | bytes 589832 | tf_op jit(solution)/shard_map/ppermute | solution.py:316
  138.6 10.5 %copy-start.1 = (bf16[2,2,192,2048]{3,2,1,0:T(8,128)(2,1)S(1)}, bf16[2,2,192,2048]{3,2,1,0:T(8,128)(2,1)}, u32[]{:S(2)}) copy-start(bf16[2,2,192,2048]{3,2,1,0:T(8,128)(2,1)} %get-tuple-element.11) | copy-start | bytes 9437188
  148.7 10.3 %collective-permute-start.6 = (bf16[384,512]{1,0:T(8,128)(2,1)}, bf16[384,512]{1,0:T(8,128)(2,1)}, u32[]{:S(2)}, u32[]{:S(2)}) collective-permute-start(bf16[384,512]{1,0:T(8,128)(2,1)} %get-tuple-element.15), channel_id=1, source_target_pairs={{0,2},{4,0},{8,4},{12,8},{14,12},{10,14},{6,10},{2,6},{1,3},{5,1},... | collective-permute-start | bytes 1179656 | tf_op jit(solution)/shard_map/ppermute | solution.py:316
  161.0 12.3 %collective-permute-start.7 = (bf16[384,512]{1,0:T(8,128)(2,1)}, bf16[384,512]{1,0:T(8,128)(2,1)}, u32[]{:S(2)}, u32[]{:S(2)}) collective-permute-start(bf16[384,512]{1,0:T(8,128)(2,1)} %add_convert_fusion.3), channel_id=1, source_target_pairs={{0,2},{4,0},{8,4},{12,8},{14,12},{10,14},{6,10},{2,6},{1,3},{5,1},... | collective-permute-start | bytes 1179656 | tf_op jit(solution)/shard_map/ppermute | solution.py:316
  172.0 14.3 %collective-permute-start.4 = (bf16[384,512]{1,0:T(8,128)(2,1)S(1)}, bf16[384,512]{1,0:T(8,128)(2,1)}, u32[]{:S(2)}, u32[]{:S(2)}) collective-permute-start(bf16[384,512]{1,0:T(8,128)(2,1)S(1)} %get-tuple-element.14), channel_id=1, source_target_pairs={{0,4},{4,8},{8,12},{12,14},{14,10},{10,6},{6,2},{2,0},{1,5},{5,9},... | collective-permute-start | bytes 1179656 | tf_op jit(solution)/shard_map/ppermute | solution.py:316
  175.3 11.0 %collective-permute-start.8 = (bf16[384,512]{1,0:T(8,128)(2,1)}, bf16[384,512]{1,0:T(8,128)(2,1)}, u32[]{:S(2)}, u32[]{:S(2)}) collective-permute-start(bf16[384,512]{1,0:T(8,128)(2,1)} %add_convert_fusion.2), channel_id=1, source_target_pairs={{0,2},{4,0},{8,4},{12,8},{14,12},{10,14},{6,10},{2,6},{1,3},{5,1},... | collective-permute-start | bytes 1179656 | tf_op jit(solution)/shard_map/ppermute | solution.py:316

commit v2 on v1

--- a/solution.py
+++ b/solution.py
@@ -36,12 +36,16 @@
     place = ring_place(n, me)
     right = ring_member(n, lax.rem(place + 1, n))
     left = ring_member(n, lax.rem(place + n - 1, n))
-    dl = xb.shape[-1]
+    dl, dh = x_in.shape[-1], x_out.shape[-1]
     rows = 4 * xb.shape[-2]
+    my_half = pl.ds(pl.multiple_of(t * dh, 128), dh)
+
+    def cell(buf, j, whose, c):
+        return buf.at[whose, c, :, pl.ds(pl.multiple_of(j * dl, 128), dl)]
 
     def own_in(arr, c):
         src, buf = ((x_in, xb), (g_in, gb))[arr]
-        return pltpu.make_async_copy(src.at[c], buf.at[me, t, c], in_sem.at[arr, c])
+        return pltpu.make_async_copy(src.at[c], cell(buf, me, t, c), in_sem.at[arr, c])
 
     for arr in range(2):
         for c in range(2):
@@ -56,14 +60,14 @@
     def hop(arr, j, s, c, way):
         buf = (xb, gb)[arr]
         return pltpu.make_async_remote_copy(
-            src_ref=buf.at[j, t, c], dst_ref=buf.at[j, t, c],
+            src_ref=cell(buf, j, t, c), dst_ref=cell(buf, j, t, c),
             send_sem=ring_send.at[arr, s - 1, c, way], recv_sem=ring_recv.at[arr, s - 1, c, way],
             device_id={"gx": (right, left)[way]}, device_id_type=MESH)
 
     def across(arr, j, c, whose):
         buf = (xb, gb)[arr]
         return pltpu.make_async_remote_copy(
-            src_ref=buf.at[j, whose, c], dst_ref=buf.at[j, whose, c],
+            src_ref=cell(buf, j, whose, c), dst_ref=cell(buf, j, whose, c),
             send_sem=sib_send.at[arr, j % half, c], recv_sem=sib_recv.at[arr, j % half, c],
             device_id={"gy": sib}, device_id_type=MESH)
 
@@ -153,12 +157,8 @@
     def tile(i):
         for which, own in ((0, a_own), (1, b_own)):
             weights(i, which).wait()
-            total = None
-            for k in range(half):
-                lhs = xb[t * half + k].reshape(rows, dl)
-                term = jnp.dot(lhs, wgu[i % 2, which, k * dl:(k + 1) * dl, :], preferred_element_type=F32)
-                total = term if total is None else total + term
-            own[i] = total
+            lhs = xb[:, :, :, my_half].reshape(rows, dh)
+            own[i] = jnp.dot(lhs, wgu[i % 2, which], preferred_element_type=F32)
             part(which, i).start()
 
             @pl.when(i + 2 < tiles)
@@ -187,14 +187,12 @@
     pl.semaphore_signal(credit, inc=1, device_id={"gy": sib}, device_id_type=MESH)
     from_sibling(1)
 
-    def outs(arr, k):
+    def outs(arr):
         buf, out = ((xb, x_out), (gb, g_out))[arr]
-        return pltpu.make_async_copy(
-            buf.at[t * half + k], out.at[:, :, :, pl.ds(k * dl, dl)], out_sem.at[arr, k])
+        return pltpu.make_async_copy(buf.at[:, :, :, my_half], out, out_sem.at[arr])
 
     for arr in range(2):
-        for k in range(half):
-            outs(arr, k).start()
+        outs(arr).start()
     pl.semaphore_wait(credit, 1)
 
     def second_half(i):
@@ -206,13 +204,8 @@
 
     def grad_tile(i, carry):
         down(i).wait()
-        total = None
-        for k in range(half):
-            lhs = gb[t * half + k].reshape(rows, dl)
-            term = lax.dot_general(lhs, wdb[i, :, k * dl:(k + 1) * dl], (((1,), (1,)), ((), ())),
-                                   preferred_element_type=F32)
-            total = term if total is None else total + term
-        a_got[i] = total
+        lhs = gb[:, :, :, my_half].reshape(rows, dh)
+        a_got[i] = lax.dot_general(lhs, wdb[i], (((1,), (1,)), ((), ())), preferred_element_type=F32)
         part(2, i).start()
 
         @pl.when(i > 0)
@@ -228,8 +221,7 @@
     lax.fori_loop(0, tiles, sent, 0)
 
     for arr in range(2):
-        for k in range(half):
-            outs(arr, k).wait()
+        outs(arr).wait()
 
         def crossed(k, carry):
             for c in range(2):
@@ -265,8 +257,8 @@
         in_specs=[anyspace] * 5,
         out_specs=(vmem, vmem, vmem, anyspace, anyspace),
         scratch_shapes=[
-            pltpu.VMEM((n, 2, 2, quarter, dl), BF16),
-            pltpu.VMEM((n, 2, 2, quarter, dl), BF16),
+            pltpu.VMEM((2, 2, quarter, n * dl), BF16),
+            pltpu.VMEM((2, 2, quarter, n * dl), BF16),
             pltpu.VMEM((2, 2, dh, width), BF16),
             pltpu.VMEM((tiles, width, dh), BF16),
             pltpu.VMEM((tiles, 2 * tok, width), F32),
@@ -282,7 +274,7 @@
             dma((2, half, 2)),
             dma((3, tiles)),
             dma((3, tiles)),
-            dma((2, half)),
+            dma((2,)),
             pltpu.SemaphoreType.REGULAR,
         ],
         compiler_params=pltpu.CompilerParams(
@@ -292,7 +284,7 @@
     )(inputs.reshape(2, quarter, dl), out_grad.reshape(2, quarter, dl), w_gate, w_up, w_down)
 
 
-def reduce_ring(n, blocks, me):
+def reduce_ring(n, blocks, me, work):
     half = n // 2
     members = [int(ring_member(n, p)) for p in range(n)]
     ways = [
@@ -301,7 +293,10 @@
     ]
     place = ring_place(n, me)
     got = [None, None]
+    at_step = {(i + 1) * half // (len(work) + 1): i for i in range(len(work))}
+    made = []
     for s in range(half):
+        sends = []
         for way in range(2):
             d = half - s
             block = blocks(ring_member(n, (place + n + (-d if way else d)) % n))
@@ -313,8 +308,17 @@
                 block = block + jnp.pad(got[way].astype(F32), (pad, (0, 0)))
             else:
                 block = block + got[way].astype(F32)
-            got[way] = lax.ppermute(block.astype(BF16), "gx", ways[way])
-    return (blocks(me) + got[0].astype(F32) + got[1].astype(F32)).astype(BF16)
+            sends.append(block.astype(BF16))
+        if s in at_step:
+            function, operand = work[at_step[s]]
+            sends[0], sends[1], operand = lax.optimization_barrier((sends[0], sends[1], operand))
+            product = function(operand)
+        got = [lax.ppermute(sends[way], "gx", ways[way]) for way in range(2)]
+        if s in at_step:
+            got[0], got[1], product = lax.optimization_barrier((got[0], got[1], product))
+            made.append(product)
+    total = (blocks(me) + got[0].astype(F32) + got[1].astype(F32)).astype(BF16)
+    return total, made
 
 
 def on_device(n, inputs, out_grad, w_gate, w_up, w_down):
@@ -341,11 +345,12 @@
         other = lax.dynamic_slice_in_dim(theirs, at, dl, 1).astype(F32)
         return jnp.where(q // half == t, own, other)
 
-    in_grad = reduce_ring(n, blocks, me)
-    tn = (((0,), (0,)), ((), ()))
-    gate_grad = lax.dot_general(xh, gt, tn, preferred_element_type=F32).astype(BF16)
-    up_grad = lax.dot_general(xh, ut, tn, preferred_element_type=F32).astype(BF16)
-    down_grad = lax.dot_general(hid, gh, tn, preferred_element_type=F32).astype(BF16)
+    def product(left):
+        return lambda right: lax.dot_general(
+            left, right, (((0,), (0,)), ((), ())), preferred_element_type=F32).astype(BF16)
+
+    in_grad, (gate_grad, up_grad, down_grad) = reduce_ring(
+        n, blocks, me, [(product(xh), gt), (product(xh), ut), (product(hid), gh)])
     return in_grad, gate_grad, up_grad, down_grad
 
 

time: 189 us -> 164 us (0.87)
  waiting for transfers between devices: 22.5 us -> 6.57 us
  other arithmetic: 12.9 us -> 8.43 us
  matrix products: 51.1 us -> 46.8 us
    ppermute x8, waiting for transfers between devices: 22.5 us -> 6.57 us  [reduce_ring(): got = [lax.ppermute(sends[way], 'gx', ways[way]) for way in range(2)]]
    convert_element_type x6 -> x4, other arithmetic: 11.1 us -> 6.53 us  [the longest x3 4.54 us: reduce_ring(): sends.append(block.astype(BF16))]
    dot_general x3, matrix products: 30.3 us -> 26 us  [product(): lax.dot_general(left, right, (((0,), (0,)), ((), ())), preferred_element_...]
  transfers between devices with their start and end apart: 9 -> 9, of which waited for: 4 -> 3; matrix products, arithmetic and copies ran while one was open for 23% -> 22% of each run, Pallas kernels for 0% -> 0%
where the time goes in v2:
time: 164 us
  Pallas kernels  91.9 us (56%)
  matrix products  46.8 us (29%)
  starting transfers between devices  8.59 us (5%)
  other arithmetic  8.43 us (5%)
  waiting for transfers between devices  6.57 us (4%)
    pallas_call x1, Pallas kernels, terms(): pl.pallas_call(functools.partial(terms_kernel, n, tiles, width), out_shap...  91.9 us
    dot_general x3, matrix products, product(): lax.dot_general(left, right, (((0,), (0,)), ((), ())), preferred_element_...  26 us
    dot_general x2, matrix products, back(): lax.dot_general(a, w_gate, nt, preferred_element_type=F32)  11.3 us
    dot_general x2, matrix products, back(): lax.dot_general(b, w_up, nt, preferred_element_type=F32)  9.46 us
    ppermute x8, starting transfers between devices, reduce_ring(): got = [lax.ppermute(sends[way], 'gx', ways[way]) for way in range(2)]  8.45 us
    ppermute x8, waiting for transfers between devices, reduce_ring(): got = [lax.ppermute(sends[way], 'gx', ways[way]) for way in range(2)]  6.57 us
    convert_element_type x3, other arithmetic, reduce_ring(): sends.append(block.astype(BF16))  4.54 us
  transfers between devices with their start and end apart: 9, of which 3 were waited for; matrix products, arithmetic and copies ran while one was open for 22% of the time, Pallas kernels for 0%

profile of v2, /device:TPU:0, one launch (start us, length us, event | category | flops | bytes accessed | tf_op | source)
XLA Modules:
  0.0 163.6 jit_solution(8644179743267390807)
XLA Ops:
  0.6 91.9 %shard_map.84 = (bf16[768,1792]{1,0:T(8,128)(2,1)}, bf16[768,1792]{1,0:T(8,128)(2,1)}, bf16[768,1792]{1,0:T(8,128)(2,1)}, bf16[2,2,192,2048]{3,2,1,0:T(8,128)(2,1)}, bf16[2,2,192,2048]{3,2,1,0:T(8,128)(2,1)}) custom-call(bf16[2,192,512]{2,1,0:T(8,128)(2,1)} %bitcast.14, bf16[2,192,512]{2,1,0:T(8,128)(2,1)} %bitcast.15, bf16[2048,1792]{1,0:T(8,128)(2,1)} %wg.1, ...), custom_call_target="tpu_custom_call" | custom-call | flops 16911433728 | bytes 36700160 | tf_op jit(solution)/shard_map/pallas_call | solution.py:254
  92.6 0.0 copy-start
  92.6 0.0 copy-start.3
  92.6 5.9 %fusion.1 = f32[384,2048]{1,0:T(8,128)S(1)} fusion(bf16[2048,1792]{1,0:T(8,128)(2,1)} %wg.1, bf16[768,1792]{1,0:T(8,128)(2,1)} %get-tuple-element.32, s32[]{:T(128)S(6)} %select_n.235), kind=kOutput, calls=%fused_computation.6 | convolution fusion | flops 2818572288 | bytes 11862020 | tf_op jit(solution)/shard_map/dot_general | solution.py:336
  98.5 0.0 copy-done
  98.5 0.5 copy-done.3
  99.0 0.0 copy-start.6
  99.0 4.1 %add_convert_fusion = bf16[384,2048]{1,0:T(8,128)(2,1)} fusion(f32[384,2048]{1,0:T(8,128)S(1)} %fusion.1, bf16[2048,1792]{1,0:T(8,128)(2,1)S(1)} %copy-done, bf16[768,1792]{1,0:T(8,128)(2,1)S(1)} %copy-done.3, s32[]{:T(128)S(6)} %select_n.235), kind=kOutput, calls=%fused_computation.3 | convolution fusion | flops 2820145152 | bytes 13434884 | tf_op jit(solution)/shard_map/dot_general | solution.py:336
  103.2 0.1 collective-permute-start
  103.3 0.0 copy-done.6
  103.3 0.0 copy-start.4
  103.3 5.4 %fusion.4 = f32[384,2048]{1,0:T(8,128)S(1)} fusion(bf16[2048,1792]{1,0:T(8,128)(2,1)} %wg.1, bf16[768,1792]{1,0:T(8,128)(2,1)S(1)} %copy-done.6, s32[]{:T(128)S(6)} %select_n.232), kind=kOutput, calls=%fused_computation.9 | convolution fusion | flops 2818572288 | bytes 11862020 | tf_op jit(solution)/shard_map/dot_general | solution.py:336
  108.7 0.0 copy-done.4
  108.8 5.3 %convolution_add_fusion = f32[384,2048]{1,0:T(8,128)S(1)} fusion(f32[384,2048]{1,0:T(8,128)S(1)} %fusion.4, bf16[2048,1792]{1,0:T(8,128)(2,1)} %wu.1, bf16[768,1792]{1,0:T(8,128)(2,1)S(1)} %copy-done.4, s32[]{:T(128)S(6)} %select_n.232), kind=kOutput, calls=%fused_computation.4 | convolution fusion | flops 2819358720 | bytes 15007748 | tf_op jit(solution)/shard_map/dot_general | solution.py:336
  114.1 0.0 collective-permute-done
  114.1 1.9 %fusion.6 = (bf16[192,512]{1,0:T(8,128)(2,1)}, bf16[192,512]{1,0:T(8,128)(2,1)}) fusion(f32[384,2048]{1,0:T(8,128)S(1)} %convolution_add_fusion, s32[]{:T(128)S(6)} %add.315, s32[]{:T(128)S(6)} %select_n.279, bf16[384,2048]{1,0:T(8,128)(2,1)} %collective-permute-done, pred[]{:T(512)S(6)} %eq.52, s32[]{:T(128)S(6)} %select_n.265, pred[]{:T(512)S(6)} %eq.50), kind=kLoop, calls=%fused_computation.19 | loop fusion | flops 393216 | bytes 1179662 | tf_op jit(solution)/shard_map/convert.4
  116.0 0.5 collective-permute-start.2
  116.5 1.6 collective-permute-start.1
  118.0 0.0 copy-start.2
  118.0 5.3 %collective-permute-done.2 = bf16[192,512]{1,0:T(8,128)(2,1)S(1)} collective-permute-done((bf16[192,512]{1,0:T(8,128)(2,1)}, bf16[192,512]{1,0:T(8,128)(2,1)S(1)}, u32[]{:S(2)}, u32[]{:S(2)}) %collective-permute-start.2) | collective-permute-done | bytes 196640 | tf_op jit(solution)/shard_map/ppermute | solution.py:316
  123.4 0.2 collective-permute-done.1
  123.6 1.4 add_convert_fusion.6
  125.0 1.8 %collective-permute-start.3 = (bf16[384,512]{1,0:T(8,128)(2,1)S(1)}, bf16[384,512]{1,0:T(8,128)(2,1)S(1)}, u32[]{:S(2)}, u32[]{:S(2)}) collective-permute-start(bf16[384,512]{1,0:T(8,128)(2,1)S(1)} %get-tuple-element.29), channel_id=1, source_target_pairs={{0,4},{4,8},{8,12},{12,14},{14,10},{10,6},{6,2},{2,0},{1,5},{5,9},... | collective-permute-start | bytes 1179656 | tf_op jit(solution)/shard_map/ppermute | solution.py:316
  126.8 0.4 collective-permute-start.4
  127.2 0.0 copy-done.2
  127.2 9.9 %convolution_convert_fusion.2 = bf16[2048,1792]{1,0:T(8,128)(2,1)} fusion(bf16[768,2048]{1,0:T(8,128)(2,1)S(1)} %bitcast.17, bf16[768,1792]{1,0:T(8,128)(2,1)} %get-tuple-element.32), kind=kOutput, calls=%fused_computation.2 | convolution fusion | flops 5640814592 | bytes 13238272 | tf_op jit(solution)/shard_map/dot_general | solution.py:349
  137.1 0.0 copy-start.5
  137.1 0.0 collective-permute-done.3
  137.1 0.0 collective-permute-done.4
  137.1 1.6 %add_convert_fusion.4 = (bf16[384,512]{1,0:T(8,128)(2,1)S(1)}, bf16[384,512]{1,0:T(8,128)(2,1)S(1)}) fusion(bf16[384,512]{1,0:T(8,128)(2,1)S(1)} %collective-permute-done.4, f32[384,2048]{1,0:T(8,128)S(1)} %convolution_add_fusion, s32[]{:T(128)S(6)} %select_n.286, bf16[384,2048]{1,0:T(8,128)(2,1)} %collective-permute-done, pred[]{:T(512)S(6)} %eq.53, ...), kind=kLoop, calls=%fused_computation.14 | loop fusion | flops 1966080 | bytes 3932170 | tf_op jit(solution)/shard_map/convert_element_type | solution.py:311
  138.7 1.7 %collective-permute-start.5 = (bf16[384,512]{1,0:T(8,128)(2,1)S(1)}, bf16[384,512]{1,0:T(8,128)(2,1)S(1)}, u32[]{:S(2)}, u32[]{:S(2)}) collective-permute-start(bf16[384,512]{1,0:T(8,128)(2,1)S(1)} %get-tuple-element.35), channel_id=1, source_target_pairs={{0,4},{4,8},{8,12},{12,14},{14,10},{10,6},{6,2},{2,0},{1,5},{5,9},... | collective-permute-start | bytes 1179656 | tf_op jit(solution)/shard_map/ppermute | solution.py:316
  140.4 0.4 collective-permute-start.6
  140.8 0.0 copy-done.5
  140.8 0.0 copy-start.7
  140.8 8.1 %convolution_convert_fusion.1 = bf16[2048,1792]{1,0:T(8,128)(2,1)} fusion(bf16[768,2048]{1,0:T(8,128)(2,1)S(1)} %bitcast.18, bf16[768,1792]{1,0:T(8,128)(2,1)S(1)} %copy-done.5), kind=kOutput, calls=%fused_computation.1 | convolution fusion | flops 5640814592 | bytes 13238272 | tf_op jit(solution)/shard_map/dot_general | solution.py:349
  148.9 0.0 copy-start.1
  148.9 0.0 collective-permute-done.5
  149.0 1.0 collective-permute-done.6
  150.0 1.5 add_convert_fusion.2
  151.5 1.6 collective-permute-start.7
  153.0 0.5 collective-permute-start.8
  153.6 0.0 copy-done.7
  153.6 0.0 copy-done.1
  153.6 8.0 %convolution_convert_fusion = bf16[1792,2048]{1,0:T(8,128)(2,1)} fusion(bf16[768,1792]{1,0:T(8,128)(2,1)S(1)} %copy-done.7, bf16[768,2048]{1,0:T(8,128)(2,1)S(1)} %bitcast.16), kind=kOutput, calls=%fused_computation | convolution fusion | flops 5640814592 | bytes 13238272 | tf_op jit(solution)/shard_map/dot_general | solution.py:349
  161.6 0.0 collective-permute-done.7
  161.6 0.0 collective-permute-done.8
  161.6 2.0 %add_convert_fusion.1 = bf16[384,512]{1,0:T(8,128)(2,1)} fusion(bf16[384,512]{1,0:T(8,128)(2,1)S(1)} %collective-permute-done.8, bf16[384,512]{1,0:T(8,128)(2,1)S(1)} %collective-permute-done.7, f32[384,2048]{1,0:T(8,128)S(1)} %convolution_add_fusion, s32[]{:T(128)S(6)} %select_n.234, bf16[384,2048]{1,0:T(8,128)(2,1)} %collective-permute-done, pred[]{:T(512)S(6)} %eq.46), kind=kLoop, calls=%fused_computation.11 | loop fusion | flops 1376256 | bytes 2359301 | tf_op jit(solution)/shard_map/convert_element_type | solution.py:320
Async XLA Ops:
  92.6 5.9 %copy-start = (bf16[2048,1792]{1,0:T(8,128)(2,1)S(1)}, bf16[2048,1792]{1,0:T(8,128)(2,1)}, u32[]{:S(2)}) copy-start(bf16[2048,1792]{1,0:T(8,128)(2,1)} %wu.1) | copy-start | bytes 22020100
  92.6 6.4 %copy-start.3 = (bf16[768,1792]{1,0:T(8,128)(2,1)S(1)}, bf16[768,1792]{1,0:T(8,128)(2,1)}, u32[]{:S(2)}) copy-start(bf16[768,1792]{1,0:T(8,128)(2,1)} %get-tuple-element.37) | copy-start | bytes 8257540
  99.0 4.3 %copy-start.6 = (bf16[768,1792]{1,0:T(8,128)(2,1)S(1)}, bf16[768,1792]{1,0:T(8,128)(2,1)}, u32[]{:S(2)}) copy-start(bf16[768,1792]{1,0:T(8,128)(2,1)} %get-tuple-element.32) | copy-start | bytes 8257540
  103.2 10.9 %collective-permute-start = (bf16[384,2048]{1,0:T(8,128)(2,1)}, bf16[384,2048]{1,0:T(8,128)(2,1)}, u32[]{:S(2)}, u32[]{:S(2)}) collective-permute-start(bf16[384,2048]{1,0:T(8,128)(2,1)} %add_convert_fusion), channel_id=1, source_target_pairs={{0,1},{1,0},{2,3},{3,2},{4,5},{5,4},{6,7},{7,6},{8,9},{9,8},{10,11... | collective-permute-start | bytes 4718600 | tf_op jit(solution)/shard_map/ppermute | solution.py:339
  103.3 5.5 %copy-start.4 = (bf16[768,1792]{1,0:T(8,128)(2,1)S(1)}, bf16[768,1792]{1,0:T(8,128)(2,1)}, u32[]{:S(2)}) copy-start(bf16[768,1792]{1,0:T(8,128)(2,1)} %get-tuple-element.37) | copy-start | bytes 8257540
  116.0 7.4 %collective-permute-start.2 = (bf16[192,512]{1,0:T(8,128)(2,1)}, bf16[192,512]{1,0:T(8,128)(2,1)S(1)}, u32[]{:S(2)}, u32[]{:S(2)}) collective-permute-start(bf16[192,512]{1,0:T(8,128)(2,1)} %get-tuple-element.56), channel_id=1, source_target_pairs={{0,2},{4,0},{8,4},{12,8},{14,12},{10,14},{6,10},{2,6},{1,3},{5,1},... | collective-permute-start | bytes 589832 | tf_op jit(solution)/shard_map/ppermute | solution.py:316
  116.5 7.1 %collective-permute-start.1 = (bf16[192,512]{1,0:T(8,128)(2,1)}, bf16[192,512]{1,0:T(8,128)(2,1)S(1)}, u32[]{:S(2)}, u32[]{:S(2)}) collective-permute-start(bf16[192,512]{1,0:T(8,128)(2,1)} %get-tuple-element.57), channel_id=1, source_target_pairs={{0,4},{4,8},{8,12},{12,14},{14,10},{10,6},{6,2},{2,0},{1,5},{5,9},... | collective-permute-start | bytes 589832 | tf_op jit(solution)/shard_map/ppermute | solution.py:316
  118.0 9.2 %copy-start.2 = (bf16[2,2,192,2048]{3,2,1,0:T(8,128)(2,1)S(1)}, bf16[2,2,192,2048]{3,2,1,0:T(8,128)(2,1)}, u32[]{:S(2)}) copy-start(bf16[2,2,192,2048]{3,2,1,0:T(8,128)(2,1)} %get-tuple-element.31) | copy-start | bytes 9437188
  125.0 12.1 %collective-permute-start.3 = (bf16[384,512]{1,0:T(8,128)(2,1)S(1)}, bf16[384,512]{1,0:T(8,128)(2,1)S(1)}, u32[]{:S(2)}, u32[]{:S(2)}) collective-permute-start(bf16[384,512]{1,0:T(8,128)(2,1)S(1)} %get-tuple-element.29), channel_id=1, source_target_pairs={{0,4},{4,8},{8,12},{12,14},{14,10},{10,6},{6,2},{2,0},{1,5},{5,9},... | collective-permute-start | bytes 1179656 | tf_op jit(solution)/shard_map/ppermute | solution.py:316
  126.8 10.3 %collective-permute-start.4 = (bf16[384,512]{1,0:T(8,128)(2,1)S(1)}, bf16[384,512]{1,0:T(8,128)(2,1)S(1)}, u32[]{:S(2)}, u32[]{:S(2)}) collective-permute-start(bf16[384,512]{1,0:T(8,128)(2,1)S(1)} %get-tuple-element.30), channel_id=1, source_target_pairs={{0,2},{4,0},{8,4},{12,8},{14,12},{10,14},{6,10},{2,6},{1,3},{5,1},... | collective-permute-start | bytes 1179656 | tf_op jit(solution)/shard_map/ppermute | solution.py:316
  137.1 3.7 %copy-start.5 = (bf16[768,1792]{1,0:T(8,128)(2,1)S(1)}, bf16[768,1792]{1,0:T(8,128)(2,1)}, u32[]{:S(2)}) copy-start(bf16[768,1792]{1,0:T(8,128)(2,1)} %get-tuple-element.37) | copy-start | bytes 8257540
  138.7 10.2 %collective-permute-start.5 = (bf16[384,512]{1,0:T(8,128)(2,1)S(1)}, bf16[384,512]{1,0:T(8,128)(2,1)S(1)}, u32[]{:S(2)}, u32[]{:S(2)}) collective-permute-start(bf16[384,512]{1,0:T(8,128)(2,1)S(1)} %get-tuple-element.35), channel_id=1, source_target_pairs={{0,4},{4,8},{8,12},{12,14},{14,10},{10,6},{6,2},{2,0},{1,5},{5,9},... | collective-permute-start | bytes 1179656 | tf_op jit(solution)/shard_map/ppermute | solution.py:316
  140.4 9.6 %collective-permute-start.6 = (bf16[384,512]{1,0:T(8,128)(2,1)S(1)}, bf16[384,512]{1,0:T(8,128)(2,1)S(1)}, u32[]{:S(2)}, u32[]{:S(2)}) collective-permute-start(bf16[384,512]{1,0:T(8,128)(2,1)S(1)} %get-tuple-element.36), channel_id=1, source_target_pairs={{0,2},{4,0},{8,4},{12,8},{14,12},{10,14},{6,10},{2,6},{1,3},{5,1},... | collective-permute-start | bytes 1179656 | tf_op jit(solution)/shard_map/ppermute | solution.py:316
  140.8 12.7 %copy-start.7 = (bf16[768,1792]{1,0:T(8,128)(2,1)S(1)}, bf16[768,1792]{1,0:T(8,128)(2,1)}, u32[]{:S(2)}) copy-start(bf16[768,1792]{1,0:T(8,128)(2,1)} %get-tuple-element.43) | copy-start | bytes 8257540
  148.9 4.6 %copy-start.1 = (bf16[2,2,192,2048]{3,2,1,0:T(8,128)(2,1)S(1)}, bf16[2,2,192,2048]{3,2,1,0:T(8,128)(2,1)}, u32[]{:S(2)}) copy-start(bf16[2,2,192,2048]{3,2,1,0:T(8,128)(2,1)} %get-tuple-element.40) | copy-start | bytes 9437188
  151.5 10.1 %collective-permute-start.7 = (bf16[384,512]{1,0:T(8,128)(2,1)S(1)}, bf16[384,512]{1,0:T(8,128)(2,1)S(1)}, u32[]{:S(2)}, u32[]{:S(2)}) collective-permute-start(bf16[384,512]{1,0:T(8,128)(2,1)S(1)} %get-tuple-element.41), channel_id=1, source_target_pairs={{0,4},{4,8},{8,12},{12,14},{14,10},{10,6},{6,2},{2,0},{1,5},{5,9},... | collective-permute-start | bytes 1179656 | tf_op jit(solution)/shard_map/ppermute | solution.py:316
  153.0 8.5 %collective-permute-start.8 = (bf16[384,512]{1,0:T(8,128)(2,1)S(1)}, bf16[384,512]{1,0:T(8,128)(2,1)S(1)}, u32[]{:S(2)}, u32[]{:S(2)}) collective-permute-start(bf16[384,512]{1,0:T(8,128)(2,1)S(1)} %get-tuple-element.42), channel_id=1, source_target_pairs={{0,2},{4,0},{8,4},{12,8},{14,12},{10,14},{6,10},{2,6},{1,3},{5,1},... | collective-permute-start | bytes 1179656 | tf_op jit(solution)/shard_map/ppermute | solution.py:316

commit v3 on v2

--- a/solution.py
+++ b/solution.py
@@ -137,8 +137,9 @@
     def x_step(e, carry):
         event(0, e)
         return carry
-    lax.fori_loop(0, 2 * (half - 1), x_step, 0)
+    lax.fori_loop(0, 2 * (half - 2), x_step, 0)
     begin(1)
+    lax.fori_loop(2 * (half - 2), 2 * (half - 1), x_step, 0)
     last_event(0)
     from_sibling(0)
 

time: 164 us -> 165 us (level)
  no operation moved by 1% of the time
where the time goes in v3:
time: 165 us
  Pallas kernels  93.4 us (57%)
  matrix products  46.8 us (28%)
  other arithmetic  8.73 us (5%)
  starting transfers between devices  8.63 us (5%)
  waiting for transfers between devices  5.93 us (4%)
    pallas_call x1, Pallas kernels, terms(): pl.pallas_call(functools.partial(terms_kernel, n, tiles, width), out_shap...  93.4 us
    dot_general x3, matrix products, product(): lax.dot_general(left, right, (((0,), (0,)), ((), ())), preferred_element_...  26 us
    dot_general x2, matrix products, back(): lax.dot_general(a, w_gate, nt, preferred_element_type=F32)  11.3 us
    dot_general x2, matrix products, back(): lax.dot_general(b, w_up, nt, preferred_element_type=F32)  9.46 us
    ppermute x8, starting transfers between devices, reduce_ring(): got = [lax.ppermute(sends[way], 'gx', ways[way]) for way in range(2)]  8.26 us
    ppermute x8, waiting for transfers between devices, reduce_ring(): got = [lax.ppermute(sends[way], 'gx', ways[way]) for way in range(2)]  5.93 us
    convert_element_type x3, other arithmetic, reduce_ring(): sends.append(block.astype(BF16))  4.85 us
  transfers between devices with their start and end apart: 9, of which 3 were waited for; matrix products, arithmetic and copies ran while one was open for 22% of the time, Pallas kernels for 0%

profile of v3, /device:TPU:0, one launch (start us, length us, event | category | flops | bytes accessed | tf_op | source)
XLA Modules:
  0.0 164.8 jit_solution(8315175185584886650)
XLA Ops:
  0.6 93.4 %shard_map.84 = (bf16[768,1792]{1,0:T(8,128)(2,1)}, bf16[768,1792]{1,0:T(8,128)(2,1)}, bf16[768,1792]{1,0:T(8,128)(2,1)}, bf16[2,2,192,2048]{3,2,1,0:T(8,128)(2,1)}, bf16[2,2,192,2048]{3,2,1,0:T(8,128)(2,1)}) custom-call(bf16[2,192,512]{2,1,0:T(8,128)(2,1)} %bitcast.14, bf16[2,192,512]{2,1,0:T(8,128)(2,1)} %bitcast.15, bf16[2048,1792]{1,0:T(8,128)(2,1)} %wg.1, ...), custom_call_target="tpu_custom_call" | custom-call | flops 16911433728 | bytes 36700160 | tf_op jit(solution)/shard_map/pallas_call | solution.py:255
  94.0 0.0 copy-start
  94.0 0.0 copy-start.3
  94.1 5.9 %fusion.1 = f32[384,2048]{1,0:T(8,128)S(1)} fusion(bf16[2048,1792]{1,0:T(8,128)(2,1)} %wg.1, bf16[768,1792]{1,0:T(8,128)(2,1)} %get-tuple-element.32, s32[]{:T(128)S(6)} %select_n.235), kind=kOutput, calls=%fused_computation.6 | convolution fusion | flops 2818572288 | bytes 11862020 | tf_op jit(solution)/shard_map/dot_general | solution.py:337
  99.9 0.0 copy-done
  100.0 0.5 copy-done.3
  100.5 0.0 copy-start.6
  100.5 4.1 %add_convert_fusion = bf16[384,2048]{1,0:T(8,128)(2,1)} fusion(f32[384,2048]{1,0:T(8,128)S(1)} %fusion.1, bf16[2048,1792]{1,0:T(8,128)(2,1)S(1)} %copy-done, bf16[768,1792]{1,0:T(8,128)(2,1)S(1)} %copy-done.3, s32[]{:T(128)S(6)} %select_n.235), kind=kOutput, calls=%fused_computation.3 | convolution fusion | flops 2820145152 | bytes 13434884 | tf_op jit(solution)/shard_map/dot_general | solution.py:337
  104.6 0.4 collective-permute-start
  105.0 0.0 copy-done.6
  105.0 0.0 copy-start.4
  105.0 5.5 %fusion.4 = f32[384,2048]{1,0:T(8,128)S(1)} fusion(bf16[2048,1792]{1,0:T(8,128)(2,1)} %wg.1, bf16[768,1792]{1,0:T(8,128)(2,1)S(1)} %copy-done.6, s32[]{:T(128)S(6)} %select_n.232), kind=kOutput, calls=%fused_computation.9 | convolution fusion | flops 2818572288 | bytes 11862020 | tf_op jit(solution)/shard_map/dot_general | solution.py:337
  110.4 0.0 copy-done.4
  110.4 5.3 %convolution_add_fusion = f32[384,2048]{1,0:T(8,128)S(1)} fusion(f32[384,2048]{1,0:T(8,128)S(1)} %fusion.4, bf16[2048,1792]{1,0:T(8,128)(2,1)} %wu.1, bf16[768,1792]{1,0:T(8,128)(2,1)S(1)} %copy-done.4, s32[]{:T(128)S(6)} %select_n.232), kind=kOutput, calls=%fused_computation.4 | convolution fusion | flops 2819358720 | bytes 15007748 | tf_op jit(solution)/shard_map/dot_general | solution.py:337
  115.8 0.0 collective-permute-done
  115.8 1.9 %fusion.6 = (bf16[192,512]{1,0:T(8,128)(2,1)}, bf16[192,512]{1,0:T(8,128)(2,1)}) fusion(f32[384,2048]{1,0:T(8,128)S(1)} %convolution_add_fusion, s32[]{:T(128)S(6)} %add.315, s32[]{:T(128)S(6)} %select_n.279, bf16[384,2048]{1,0:T(8,128)(2,1)} %collective-permute-done, pred[]{:T(512)S(6)} %eq.52, s32[]{:T(128)S(6)} %select_n.265, pred[]{:T(512)S(6)} %eq.50), kind=kLoop, calls=%fused_computation.19 | loop fusion | flops 393216 | bytes 1179662 | tf_op jit(solution)/shard_map/convert.4
  117.7 0.4 collective-permute-start.2
  118.1 1.6 collective-permute-start.1
  119.7 0.0 copy-start.2
  119.7 5.1 %collective-permute-done.2 = bf16[192,512]{1,0:T(8,128)(2,1)S(1)} collective-permute-done((bf16[192,512]{1,0:T(8,128)(2,1)}, bf16[192,512]{1,0:T(8,128)(2,1)S(1)}, u32[]{:S(2)}, u32[]{:S(2)}) %collective-permute-start.2) | collective-permute-done | bytes 196640 | tf_op jit(solution)/shard_map/ppermute | solution.py:317
  124.8 0.2 collective-permute-done.1
  125.0 1.4 add_convert_fusion.6
  126.4 1.6 collective-permute-start.3
  128.1 0.4 collective-permute-start.4
  128.5 0.0 copy-done.2
  128.5 9.9 %convolution_convert_fusion.2 = bf16[2048,1792]{1,0:T(8,128)(2,1)} fusion(bf16[768,2048]{1,0:T(8,128)(2,1)S(1)} %bitcast.17, bf16[768,1792]{1,0:T(8,128)(2,1)} %get-tuple-element.32), kind=kOutput, calls=%fused_computation.2 | convolution fusion | flops 5640814592 | bytes 13238272 | tf_op jit(solution)/shard_map/dot_general | solution.py:350
  138.4 0.0 copy-start.5
  138.4 0.0 collective-permute-done.3
  138.4 0.0 collective-permute-done.4
  138.4 1.6 %add_convert_fusion.4 = (bf16[384,512]{1,0:T(8,128)(2,1)S(1)}, bf16[384,512]{1,0:T(8,128)(2,1)S(1)}) fusion(bf16[384,512]{1,0:T(8,128)(2,1)S(1)} %collective-permute-done.4, f32[384,2048]{1,0:T(8,128)S(1)} %convolution_add_fusion, s32[]{:T(128)S(6)} %select_n.286, bf16[384,2048]{1,0:T(8,128)(2,1)} %collective-permute-done, pred[]{:T(512)S(6)} %eq.53, ...), kind=kLoop, calls=%fused_computation.14 | loop fusion | flops 1966080 | bytes 3932170 | tf_op jit(solution)/shard_map/convert_element_type | solution.py:312
  140.0 1.6 collective-permute-start.5
  141.7 0.5 collective-permute-start.6
  142.1 0.0 copy-done.5
  142.1 0.0 copy-start.7
  142.1 8.1 %convolution_convert_fusion.1 = bf16[2048,1792]{1,0:T(8,128)(2,1)} fusion(bf16[768,2048]{1,0:T(8,128)(2,1)S(1)} %bitcast.18, bf16[768,1792]{1,0:T(8,128)(2,1)S(1)} %copy-done.5), kind=kOutput, calls=%fused_computation.1 | convolution fusion | flops 5640814592 | bytes 13238272 | tf_op jit(solution)/shard_map/dot_general | solution.py:350
  150.2 0.0 copy-start.1
  150.2 0.0 collective-permute-done.5
  150.3 0.6 collective-permute-done.6
  150.9 1.8 %add_convert_fusion.2 = (bf16[384,512]{1,0:T(8,128)(2,1)S(1)}, bf16[384,512]{1,0:T(8,128)(2,1)S(1)}) fusion(bf16[384,512]{1,0:T(8,128)(2,1)S(1)} %collective-permute-done.6, f32[384,2048]{1,0:T(8,128)S(1)} %convolution_add_fusion, s32[]{:T(128)S(6)} %select_n.293, bf16[384,2048]{1,0:T(8,128)(2,1)} %collective-permute-done, pred[]{:T(512)S(6)} %eq.54, ...), kind=kLoop, calls=%fused_computation.12 | loop fusion | flops 1966080 | bytes 3932170 | tf_op jit(solution)/shard_map/convert_element_type | solution.py:312
  152.7 1.5 collective-permute-start.7
  154.1 0.6 collective-permute-start.8
  154.7 0.0 copy-done.7
  154.7 0.0 copy-done.1
  154.7 8.0 %convolution_convert_fusion = bf16[1792,2048]{1,0:T(8,128)(2,1)} fusion(bf16[768,1792]{1,0:T(8,128)(2,1)S(1)} %copy-done.7, bf16[768,2048]{1,0:T(8,128)(2,1)S(1)} %bitcast.16), kind=kOutput, calls=%fused_computation | convolution fusion | flops 5640814592 | bytes 13238272 | tf_op jit(solution)/shard_map/dot_general | solution.py:350
  162.8 0.0 collective-permute-done.7
  162.8 0.0 collective-permute-done.8
  162.8 2.0 %add_convert_fusion.1 = bf16[384,512]{1,0:T(8,128)(2,1)} fusion(bf16[384,512]{1,0:T(8,128)(2,1)S(1)} %collective-permute-done.8, bf16[384,512]{1,0:T(8,128)(2,1)S(1)} %collective-permute-done.7, f32[384,2048]{1,0:T(8,128)S(1)} %convolution_add_fusion, s32[]{:T(128)S(6)} %select_n.234, bf16[384,2048]{1,0:T(8,128)(2,1)} %collective-permute-done, pred[]{:T(512)S(6)} %eq.46), kind=kLoop, calls=%fused_computation.11 | loop fusion | flops 1376256 | bytes 2359301 | tf_op jit(solution)/shard_map/convert_element_type | solution.py:321
Async XLA Ops:
  94.0 5.9 %copy-start = (bf16[2048,1792]{1,0:T(8,128)(2,1)S(1)}, bf16[2048,1792]{1,0:T(8,128)(2,1)}, u32[]{:S(2)}) copy-start(bf16[2048,1792]{1,0:T(8,128)(2,1)} %wu.1) | copy-start | bytes 22020100
  94.0 6.4 %copy-start.3 = (bf16[768,1792]{1,0:T(8,128)(2,1)S(1)}, bf16[768,1792]{1,0:T(8,128)(2,1)}, u32[]{:S(2)}) copy-start(bf16[768,1792]{1,0:T(8,128)(2,1)} %get-tuple-element.37) | copy-start | bytes 8257540
  100.5 4.5 %copy-start.6 = (bf16[768,1792]{1,0:T(8,128)(2,1)S(1)}, bf16[768,1792]{1,0:T(8,128)(2,1)}, u32[]{:S(2)}) copy-start(bf16[768,1792]{1,0:T(8,128)(2,1)} %get-tuple-element.32) | copy-start | bytes 8257540
  104.6 11.2 %collective-permute-start = (bf16[384,2048]{1,0:T(8,128)(2,1)}, bf16[384,2048]{1,0:T(8,128)(2,1)}, u32[]{:S(2)}, u32[]{:S(2)}) collective-permute-start(bf16[384,2048]{1,0:T(8,128)(2,1)} %add_convert_fusion), channel_id=1, source_target_pairs={{0,1},{1,0},{2,3},{3,2},{4,5},{5,4},{6,7},{7,6},{8,9},{9,8},{10,11... | collective-permute-start | bytes 4718600 | tf_op jit(solution)/shard_map/ppermute | solution.py:340
  105.0 5.5 %copy-start.4 = (bf16[768,1792]{1,0:T(8,128)(2,1)S(1)}, bf16[768,1792]{1,0:T(8,128)(2,1)}, u32[]{:S(2)}) copy-start(bf16[768,1792]{1,0:T(8,128)(2,1)} %get-tuple-element.37) | copy-start | bytes 8257540
  117.7 7.1 %collective-permute-start.2 = (bf16[192,512]{1,0:T(8,128)(2,1)}, bf16[192,512]{1,0:T(8,128)(2,1)S(1)}, u32[]{:S(2)}, u32[]{:S(2)}) collective-permute-start(bf16[192,512]{1,0:T(8,128)(2,1)} %get-tuple-element.56), channel_id=1, source_target_pairs={{0,2},{4,0},{8,4},{12,8},{14,12},{10,14},{6,10},{2,6},{1,3},{5,1},... | collective-permute-start | bytes 589832 | tf_op jit(solution)/shard_map/ppermute | solution.py:317
  118.1 6.9 %collective-permute-start.1 = (bf16[192,512]{1,0:T(8,128)(2,1)}, bf16[192,512]{1,0:T(8,128)(2,1)S(1)}, u32[]{:S(2)}, u32[]{:S(2)}) collective-permute-start(bf16[192,512]{1,0:T(8,128)(2,1)} %get-tuple-element.57), channel_id=1, source_target_pairs={{0,4},{4,8},{8,12},{12,14},{14,10},{10,6},{6,2},{2,0},{1,5},{5,9},... | collective-permute-start | bytes 589832 | tf_op jit(solution)/shard_map/ppermute | solution.py:317
  119.7 8.8 %copy-start.2 = (bf16[2,2,192,2048]{3,2,1,0:T(8,128)(2,1)S(1)}, bf16[2,2,192,2048]{3,2,1,0:T(8,128)(2,1)}, u32[]{:S(2)}) copy-start(bf16[2,2,192,2048]{3,2,1,0:T(8,128)(2,1)} %get-tuple-element.31) | copy-start | bytes 9437188
  126.4 12.0 %collective-permute-start.3 = (bf16[384,512]{1,0:T(8,128)(2,1)S(1)}, bf16[384,512]{1,0:T(8,128)(2,1)S(1)}, u32[]{:S(2)}, u32[]{:S(2)}) collective-permute-start(bf16[384,512]{1,0:T(8,128)(2,1)S(1)} %get-tuple-element.29), channel_id=1, source_target_pairs={{0,4},{4,8},{8,12},{12,14},{14,10},{10,6},{6,2},{2,0},{1,5},{5,9},... | collective-permute-start | bytes 1179656 | tf_op jit(solution)/shard_map/ppermute | solution.py:317
  128.1 10.3 %collective-permute-start.4 = (bf16[384,512]{1,0:T(8,128)(2,1)S(1)}, bf16[384,512]{1,0:T(8,128)(2,1)S(1)}, u32[]{:S(2)}, u32[]{:S(2)}) collective-permute-start(bf16[384,512]{1,0:T(8,128)(2,1)S(1)} %get-tuple-element.30), channel_id=1, source_target_pairs={{0,2},{4,0},{8,4},{12,8},{14,12},{10,14},{6,10},{2,6},{1,3},{5,1},... | collective-permute-start | bytes 1179656 | tf_op jit(solution)/shard_map/ppermute | solution.py:317
  138.4 3.7 %copy-start.5 = (bf16[768,1792]{1,0:T(8,128)(2,1)S(1)}, bf16[768,1792]{1,0:T(8,128)(2,1)}, u32[]{:S(2)}) copy-start(bf16[768,1792]{1,0:T(8,128)(2,1)} %get-tuple-element.37) | copy-start | bytes 8257540
  140.0 10.2 %collective-permute-start.5 = (bf16[384,512]{1,0:T(8,128)(2,1)S(1)}, bf16[384,512]{1,0:T(8,128)(2,1)S(1)}, u32[]{:S(2)}, u32[]{:S(2)}) collective-permute-start(bf16[384,512]{1,0:T(8,128)(2,1)S(1)} %get-tuple-element.35), channel_id=1, source_target_pairs={{0,4},{4,8},{8,12},{12,14},{14,10},{10,6},{6,2},{2,0},{1,5},{5,9},... | collective-permute-start | bytes 1179656 | tf_op jit(solution)/shard_map/ppermute | solution.py:317
  141.7 9.2 %collective-permute-start.6 = (bf16[384,512]{1,0:T(8,128)(2,1)S(1)}, bf16[384,512]{1,0:T(8,128)(2,1)S(1)}, u32[]{:S(2)}, u32[]{:S(2)}) collective-permute-start(bf16[384,512]{1,0:T(8,128)(2,1)S(1)} %get-tuple-element.36), channel_id=1, source_target_pairs={{0,2},{4,0},{8,4},{12,8},{14,12},{10,14},{6,10},{2,6},{1,3},{5,1},... | collective-permute-start | bytes 1179656 | tf_op jit(solution)/shard_map/ppermute | solution.py:317
  142.1 12.6 %copy-start.7 = (bf16[768,1792]{1,0:T(8,128)(2,1)S(1)}, bf16[768,1792]{1,0:T(8,128)(2,1)}, u32[]{:S(2)}) copy-start(bf16[768,1792]{1,0:T(8,128)(2,1)} %get-tuple-element.43) | copy-start | bytes 8257540
  150.2 4.5 %copy-start.1 = (bf16[2,2,192,2048]{3,2,1,0:T(8,128)(2,1)S(1)}, bf16[2,2,192,2048]{3,2,1,0:T(8,128)(2,1)}, u32[]{:S(2)}) copy-start(bf16[2,2,192,2048]{3,2,1,0:T(8,128)(2,1)} %get-tuple-element.40) | copy-start | bytes 9437188
  152.7 10.1 %collective-permute-start.7 = (bf16[384,512]{1,0:T(8,128)(2,1)S(1)}, bf16[384,512]{1,0:T(8,128)(2,1)S(1)}, u32[]{:S(2)}, u32[]{:S(2)}) collective-permute-start(bf16[384,512]{1,0:T(8,128)(2,1)S(1)} %get-tuple-element.41), channel_id=1, source_target_pairs={{0,4},{4,8},{8,12},{12,14},{14,10},{10,6},{6,2},{2,0},{1,5},{5,9},... | collective-permute-start | bytes 1179656 | tf_op jit(solution)/shard_map/ppermute | solution.py:317
  154.1 8.7 %collective-permute-start.8 = (bf16[384,512]{1,0:T(8,128)(2,1)S(1)}, bf16[384,512]{1,0:T(8,128)(2,1)S(1)}, u32[]{:S(2)}, u32[]{:S(2)}) collective-permute-start(bf16[384,512]{1,0:T(8,128)(2,1)S(1)} %get-tuple-element.42), channel_id=1, source_target_pairs={{0,2},{4,0},{8,4},{12,8},{14,12},{10,14},{6,10},{2,6},{1,3},{5,1},... | collective-permute-start | bytes 1179656 | tf_op jit(solution)/shard_map/ppermute | solution.py:317
